TPU v7x, 512 devices: a whole 4x8x8 slice. The times are simulated.
512 devices in a mesh: pipe: 4 (over x), rep: 4 (over y_lo, core), ep: 32 (over z, y_hi).
Axes of the slice: x: 4, y: 8 (y_hi: 4, y_lo: 2; y = y_hi * 2 + y_lo), z: 8, core: 2. Of those that a mesh axis runs over, the one named last changes fastest.
Arguments:
- a_sent: bfloat16 [4, 4096, 3584], P('pipe', 'ep', 'rep'), may hold values from -6 to 6
- b_input: bfloat16 [4, 4096, 3584], P('pipe', 'ep', 'rep'), may hold values from -6 to 6
- b_grad: bfloat16 [4, 4096, 3584], P('pipe', 'ep', 'rep'), may hold values from -6 to 6
- routes_a: int32 [4, 4096, 8], P('pipe', 'ep'), may hold values from 0 to 255, all different within a row; in each aligned block of 128 rows (0 to 127, 128 to 255, ..., all dimensions but the last counted through in order) at most 8 rows name the same one
- routes_b: int32 [4, 4096, 8], P('pipe', 'ep'), may hold values from 0 to 255, all different within a row; in each aligned block of 128 rows (0 to 127, 128 to 255, ..., all dimensions but the last counted through in order) at most 8 rows name the same one
- gates_a: bfloat16 [4, 4096, 8], P('pipe', 'ep'), may hold values from 0.049804688 to 0.59765625
- gates_b: bfloat16 [4, 4096, 8], P('pipe', 'ep'), may hold values from 0.049804688 to 0.59765625
- w_in: bfloat16 [4, 32, 3584, 4, 256], P('pipe', 'ep', None, 'rep'), may hold values from -0.09375 to 0.09375
- w_down: bfloat16 [4, 32, 3584, 4, 128], P('pipe', 'ep', None, 'rep'), may hold values from -0.1875 to 0.1875
Outputs:
- y_a: bfloat16 [4, 4096, 3584], P('pipe', 'ep', 'rep')
- dx_b: bfloat16 [4, 4096, 3584], P('pipe', 'ep', 'rep')
- dgate_b: bfloat16 [4, 4096, 8], P('pipe', 'ep')
Inputs may be any that keep to these rules, and one draw needn't show every extreme that they name: `routes_a`: each row names 8 different numbers; in the rows of one device no number is named by more than 8 rows. `routes_b`: each row names 8 different numbers; in the rows of one device no number is named by more than 8 rows.
All inputs are finite; a program needn't handle non-finite values.
Results may differ from a plain program's by a relative error of at most 0.015.
Values may be sent and summed in bfloat16 or wider, within the bound.
No kernel may reach another device: no remote copies, remote signals or barrier semaphores. Data moves between devices by JAX's collectives and lax.ppermute only.
A program may use at most 64 MiB of HBM per device.

v0:
```python
import jax
import jax.numpy as jnp
from jax import lax
from jax.sharding import PartitionSpec as P

CAP = 8


HIGH = lax.Precision.HIGHEST


def passed_along(value, axis, by):
    size = lax.axis_size(axis)
    return lax.ppermute(value, axis, [(i, (i + by) % size) for i in range(size)])


def tables(routes, gates, experts_total, depth):
    matches = (routes[..., None] == jnp.arange(experts_total, dtype=jnp.int32)).astype(jnp.int32)
    hit_count = jnp.sum(matches, axis=2)
    weight = jnp.sum(gates.astype(jnp.float32)[..., None] * matches.astype(jnp.float32), axis=2)
    before = jnp.cumsum(hit_count, axis=1) - hit_count
    select = hit_count[..., None] * (
        before[..., None] == jnp.arange(depth, dtype=jnp.int32)
    ).astype(jnp.int32)
    return (matches, select.astype(jnp.float32), weight)


def pick_rows(select, values):
    picked = jnp.einsum(
        "btec,btd->becd", select.astype(jnp.bfloat16), values, preferred_element_type=jnp.float32
    )
    return jnp.repeat(picked[0].astype(jnp.bfloat16), 2, axis=0)


def block_forward(rows, w_block, down_block):
    units = down_block.shape[1]
    gate_up = jnp.dot(rows, w_block, preferred_element_type=jnp.float32)
    hidden = (jax.nn.silu(gate_up[:, :units]) * gate_up[:, units:]).astype(jnp.bfloat16)
    output = lax.dot_general(
        hidden, down_block, (((1,), (1,)), ((), ())), preferred_element_type=jnp.float32
    )
    return (gate_up, output)


def block_backward(gate_up, d_out, w_block, down_block):
    units = down_block.shape[1]
    gate_part, up_part = (gate_up[:, :units], gate_up[:, units:])
    d_hidden = jnp.dot(d_out, down_block, preferred_element_type=jnp.float32)
    squash = jax.nn.sigmoid(gate_part)
    d_gate = (d_hidden * up_part * squash * (1.0 + gate_part * (1.0 - squash))).astype(jnp.bfloat16)
    d_up = (d_hidden * gate_part * squash).astype(jnp.bfloat16)
    d_gate_up = jnp.concatenate([d_gate, d_up], axis=1)
    d_rows = lax.dot_general(
        d_gate_up, w_block, (((1,), (1,)), ((), ())), preferred_element_type=jnp.float32
    )
    return d_rows.astype(jnp.bfloat16)


def on_device(a_sent, b_input, b_grad, routes_a, routes_b, gates_a, gates_b, w_in, w_down):
    experts = lax.axis_size("ep") // 2
    input_a = passed_along(a_sent, "pipe", 1)
    match_a, select_a, weight_a = tables(routes_a, gates_a, experts, CAP)
    match_b, select_b, weight_b = tables(routes_b, gates_b, experts, CAP)
    slot_gate = jnp.einsum("btec,bte->bec", select_b, weight_b, precision=HIGH)[0].astype(
        jnp.bfloat16
    )
    slot_gate = jnp.repeat(slot_gate, 2, axis=0)
    full_a, full_b, full_g = (
        lax.all_gather(input_a, "rep", axis=2, tiled=True),
        lax.all_gather(b_input, "rep", axis=2, tiled=True),
        lax.all_gather(b_grad, "rep", axis=2, tiled=True),
    )
    recv_a, recv_b, recv_g, recv_gate = (
        lax.all_to_all(pick_rows(select_a, full_a), "ep", split_axis=0, concat_axis=0, tiled=True),
        lax.all_to_all(pick_rows(select_b, full_b), "ep", split_axis=0, concat_axis=0, tiled=True),
        lax.all_to_all(pick_rows(select_b, full_g), "ep", split_axis=0, concat_axis=0, tiled=True),
        lax.all_to_all(slot_gate, "ep", split_axis=0, concat_axis=0, tiled=True),
    )
    sources, depth, width = recv_a.shape
    rows_a = recv_a.reshape(-1, width)
    rows_b = recv_b.reshape(-1, width)
    grads_wide = recv_g.reshape(-1, width).astype(jnp.float32)
    w_block = w_in[0, 0, :, 0, :]
    down_block = w_down[0, 0, :, 0, :]
    output_a = block_forward(rows_a, w_block, down_block)[1].astype(jnp.bfloat16)
    gate_up_b, output_b = block_forward(rows_b, w_block, down_block)
    gate_terms = jnp.sum(output_b * grads_wide, axis=1)
    d_out = (recv_gate.reshape(-1).astype(jnp.float32)[:, None] * grads_wide).astype(jnp.bfloat16)
    dx_part = block_backward(gate_up_b, d_out, w_block, down_block)
    sum_a, sum_dx = (
        lax.psum_scatter(output_a, "rep", scatter_dimension=1, tiled=True).astype(jnp.float32),
        lax.psum_scatter(dx_part, "rep", scatter_dimension=1, tiled=True).astype(jnp.float32),
    )
    sum_dg = lax.psum(gate_terms, "rep")
    half_a = sum_a.astype(jnp.bfloat16).reshape(sources, depth, -1)
    half_dx = sum_dx.astype(jnp.bfloat16).reshape(sources, depth, -1)
    half_dg = sum_dg.astype(jnp.bfloat16).reshape(sources, depth)
    back_a, back_dx, back_dg = (
        lax.all_to_all(half_a, "ep", split_axis=0, concat_axis=0, tiled=True),
        lax.all_to_all(half_dx, "ep", split_axis=0, concat_axis=0, tiled=True),
        lax.all_to_all(half_dg, "ep", split_axis=0, concat_axis=0, tiled=True),
    )
    back_a = back_a.astype(jnp.float32).reshape(experts, 2, depth, -1)
    back_dx = back_dx.astype(jnp.float32).reshape(experts, 2, depth, -1)
    back_dg = back_dg.astype(jnp.float32).reshape(experts, 2, depth)
    combined = jnp.einsum(
        "tec,ehcd->td", (select_a * weight_a[..., None])[0], back_a, precision=HIGH
    )
    grad_in = jnp.einsum("tec,ehcd->td", select_b[0], back_dx, precision=HIGH)
    per_expert = jnp.einsum("tec,ehc->te", select_b[0], back_dg, precision=HIGH)
    dgate = jnp.sum(match_b[0].astype(jnp.float32) * per_expert[:, None, :], axis=2)
    return (
        combined.astype(jnp.bfloat16)[None],
        grad_in.astype(jnp.bfloat16)[None],
        dgate.astype(jnp.bfloat16)[None],
    )


def solution(mesh):
    placed = (
        P("pipe", "ep", "rep"),
        P("pipe", "ep", "rep"),
        P("pipe", "ep", "rep"),
        P("pipe", "ep", None),
        P("pipe", "ep", None),
        P("pipe", "ep", None),
        P("pipe", "ep", None),
        P("pipe", "ep", None, "rep", None),
        P("pipe", "ep", None, "rep", None),
    )
    return jax.shard_map(
        on_device,
        mesh=mesh,
        in_specs=placed,
        out_specs=(P("pipe", "ep", "rep"), P("pipe", "ep", "rep"), P("pipe", "ep", None)),
        check_vma=False,
    )
```

profile of v0, /device:TPU:2, one launch (start us, length us, event | category | flops | bytes accessed | tf_op | source)
XLA Modules:
  0.0 348.9 jit_solution(2641458565781782004)
XLA Ops:
  10.7 16.0 %all-to-all-start.2 = ((bf16[32,1,8]{2,1,0:T(2,128)(2,1)}), bf16[32,1,8]{2,1,0:T(2,128)(2,1)S(1)}, u32[]{:S(2)}, u32[]{:S(2)}) async-start(bf16[32,1,8]{2,1,0:T(2,128)(2,1)} %copy.91), calls=%async_computation.2 | async-start | bytes 32768 | tf_op jit(solution)/shard_map/all_to_all | solution.py:77
  26.7 8.9 %all_gather.11 = bf16[1,128,3584]{2,1,0:T(8,128)(2,1)S(1)} all-gather(bf16[1,128,896]{2,1,0:T(8,128)(2,1)} %param.10), channel_id=1, replica_groups=mesh['pipe'=4,'rep'=4,'ep'=32] {'rep'}, dimensions={2}, use_global_device_ids=true | all-gather | bytes 1146880 | tf_op jit(solution)/shard_map/all_gather | solution.py:70
  36.0 2.7 all-to-all-done.2
  40.1 9.5 %all-to-all-start.4 = ((bf16[32,8,3584]{2,1,0:T(8,128)(2,1)}), bf16[32,8,3584]{2,1,0:T(8,128)(2,1)}, u32[]{:S(2)}, u32[]{:S(2)}) async-start(bf16[32,8,3584]{2,1,0:T(8,128)(2,1)} %bitcast.108), calls=%async_computation.4 | async-start | bytes 3670016 | tf_op jit(solution)/shard_map/all_to_all | solution.py:75
  49.6 48.8 %all_gather.10 = bf16[1,128,3584]{2,1,0:T(8,128)(2,1)S(1)} all-gather(bf16[1,128,896]{2,1,0:T(8,128)(2,1)S(1)} %copy-done.2), channel_id=1, replica_groups=mesh['pipe'=4,'rep'=4,'ep'=32] {'rep'}, dimensions={2}, use_global_device_ids=true | all-gather | bytes 1146880 | tf_op jit(solution)/shard_map/all_gather | solution.py:71
  100.3 9.9 %all-to-all-start.3 = ((bf16[32,8,3584]{2,1,0:T(8,128)(2,1)}), bf16[32,8,3584]{2,1,0:T(8,128)(2,1)}, u32[]{:S(2)}, u32[]{:S(2)}) async-start(bf16[32,8,3584]{2,1,0:T(8,128)(2,1)} %bitcast.106), calls=%async_computation.3 | async-start | bytes 3670016 | tf_op jit(solution)/shard_map/all_to_all | solution.py:76
  110.2 3.4 collective-permute-start
  114.0 5.6 %collective-permute-done = bf16[1,128,896]{2,1,0:T(8,128)(2,1)S(1)} collective-permute-done((bf16[1,128,896]{2,1,0:T(8,128)(2,1)S(1)}, bf16[1,128,896]{2,1,0:T(8,128)(2,1)S(1)}, u32[]{:S(2)}, u32[]{:S(2)}) %collective-permute-start) | collective-permute-done | bytes 229408 | tf_op jit(solution)/shard_map/ppermute | solution.py:14
  119.6 42.2 %all_gather.9 = bf16[1,128,3584]{2,1,0:T(8,128)(2,1)S(1)} all-gather(bf16[1,128,896]{2,1,0:T(8,128)(2,1)S(1)} %collective-permute-done), channel_id=1, replica_groups=mesh['pipe'=4,'rep'=4,'ep'=32] {'rep'}, dimensions={2}, use_global_device_ids=true | all-gather | bytes 1146880 | tf_op jit(solution)/shard_map/all_gather | solution.py:69
  162.2 2.1 fusion.4
  165.8 18.2 %all-to-all-start = ((bf16[32,8,3584]{2,1,0:T(8,128)(2,1)}), bf16[32,8,3584]{2,1,0:T(8,128)(2,1)}, u32[]{:S(2)}, u32[]{:S(2)}) async-start(bf16[32,8,3584]{2,1,0:T(8,128)(2,1)} %bitcast.107), calls=%async_computation | async-start | bytes 3670016 | tf_op jit(solution)/shard_map/all_to_all | solution.py:74
  184.1 2.2 multiply_convert_fusion.2
  188.3 3.8 %copy.109 = bf16[256,3584]{0,1:T(8,128)(2,1)} copy(bf16[256,3584]{1,0:T(8,128)(2,1)} %convolution_convert_fusion.1) | data formatting | bytes 3670016
  192.2 56.9 %all-to-all-done = bf16[32,8,3584]{2,1,0:T(8,128)(2,1)} async-done(((bf16[32,8,3584]{2,1,0:T(8,128)(2,1)}), bf16[32,8,3584]{2,1,0:T(8,128)(2,1)}, u32[]{:S(2)}, u32[]{:S(2)}) %all-to-all-start) | async-done | bytes 1835040 | tf_op jit(solution)/shard_map/all_to_all | solution.py:74
  249.1 2.1 fusion.8
  253.2 3.8 %copy.107 = bf16[256,3584]{0,1:T(8,128)(2,1)} copy(bf16[256,3584]{1,0:T(8,128)(2,1)} %convolution_convert_fusion) | data formatting | bytes 3670016
  257.0 2.2 fusion.12
  259.2 5.8 %psum.7 = bf16[256]{0:T(256)(128)(2,1)S(1)} all-reduce(f32[256]{0:T(256)S(1)} %fusion.12), channel_id=1, replica_groups=mesh['pipe'=4,'rep'=4,'ep'=32] {'rep'}, use_global_device_ids=true, to_apply=%region_11.12 | all-reduce | flops 256 | bytes 1536 | tf_op jit(solution)/shard_map/psum | solution.py:94
  265.7 17.9 %all-to-all-start.6 = ((bf16[32,1,8]{2,1,0:T(2,128)(2,1)}), bf16[32,1,8]{2,1,0:T(2,128)(2,1)S(1)}, u32[]{:S(2)}, u32[]{:S(2)}) async-start(bf16[32,1,8]{2,1,0:T(2,128)(2,1)} %all_to_all.36), calls=%async_computation.6 | async-start | bytes 32768 | tf_op jit(solution)/shard_map/all_to_all | solution.py:101
  285.7 10.2 %all-to-all-done.6 = bf16[32,1,8]{2,1,0:T(2,128)(2,1)S(1)} async-done(((bf16[32,1,8]{2,1,0:T(2,128)(2,1)}), bf16[32,1,8]{2,1,0:T(2,128)(2,1)S(1)}, u32[]{:S(2)}, u32[]{:S(2)}) %all-to-all-start.6) | async-done | bytes 544 | tf_op jit(solution)/shard_map/all_to_all | solution.py:101
  295.9 3.9 %all-to-all-start.5 = ((bf16[32,8,896]{2,1,0:T(8,128)(2,1)}), bf16[32,8,896]{2,1,0:T(8,128)(2,1)S(1)}, u32[]{:S(2)}, u32[]{:S(2)}) async-start(bf16[32,8,896]{2,1,0:T(8,128)(2,1)} %bitcast.28), calls=%async_computation.5 | async-start | bytes 917504 | tf_op jit(solution)/shard_map/all_to_all | solution.py:100
  301.8 14.9 %all-to-all-done.5 = bf16[32,8,896]{2,1,0:T(8,128)(2,1)S(1)} async-done(((bf16[32,8,896]{2,1,0:T(8,128)(2,1)}), bf16[32,8,896]{2,1,0:T(8,128)(2,1)S(1)}, u32[]{:S(2)}, u32[]{:S(2)}) %all-to-all-start.5) | async-done | bytes 458784 | tf_op jit(solution)/shard_map/all_to_all | solution.py:100
  316.8 6.1 %all-to-all-start.1 = ((bf16[32,8,896]{2,1,0:T(8,128)(2,1)}), bf16[32,8,896]{2,1,0:T(8,128)(2,1)S(1)}, u32[]{:S(2)}, u32[]{:S(2)}) async-start(bf16[32,8,896]{2,1,0:T(8,128)(2,1)} %bitcast.8), calls=%async_computation.1 | async-start | bytes 917504 | tf_op jit(solution)/shard_map/all_to_all | solution.py:99
  325.2 15.5 %all-to-all-done.1 = bf16[32,8,896]{2,1,0:T(8,128)(2,1)S(1)} async-done(((bf16[32,8,896]{2,1,0:T(8,128)(2,1)}), bf16[32,8,896]{2,1,0:T(8,128)(2,1)S(1)}, u32[]{:S(2)}, u32[]{:S(2)}) %all-to-all-start.1) | async-done | bytes 458784 | tf_op jit(solution)/shard_map/all_to_all | solution.py:99
  (62 shorter events, 21.7 us)
Async XLA Ops:
  7.2 155.1 %copy-start = (bf16[1,1,3584,1,256]{4,2,3,1,0:T(8,128)(2,1)S(1)}, bf16[1,1,3584,1,256]{4,2,3,1,0:T(8,128)(2,1)}, u32[]{:S(2)}) copy-start(bf16[1,1,3584,1,256]{4,2,3,1,0:T(8,128)(2,1)} %param.16) | copy-start | bytes 5505028
  10.7 28.1 %all-to-all-start.2 = ((bf16[32,1,8]{2,1,0:T(2,128)(2,1)}), bf16[32,1,8]{2,1,0:T(2,128)(2,1)S(1)}, u32[]{:S(2)}, u32[]{:S(2)}) async-start(bf16[32,1,8]{2,1,0:T(2,128)(2,1)} %copy.91), calls=%async_computation.2 | async-start | bytes 32768 | tf_op jit(solution)/shard_map/all_to_all | solution.py:77
  40.1 9.5 %copy-start.2 = (bf16[1,128,896]{2,1,0:T(8,128)(2,1)S(1)}, bf16[1,128,896]{2,1,0:T(8,128)(2,1)}, u32[]{:S(2)}) copy-start(bf16[1,128,896]{2,1,0:T(8,128)(2,1)} %param.11) | copy-start | bytes 688132
  40.1 58.7 %all-to-all-start.4 = ((bf16[32,8,3584]{2,1,0:T(8,128)(2,1)}), bf16[32,8,3584]{2,1,0:T(8,128)(2,1)}, u32[]{:S(2)}, u32[]{:S(2)}) async-start(bf16[32,8,3584]{2,1,0:T(8,128)(2,1)} %bitcast.108), calls=%async_computation.4 | async-start | bytes 3670016 | tf_op jit(solution)/shard_map/all_to_all | solution.py:75
  100.3 9.9 %copy-start.6 = (bf16[1,128,896]{2,1,0:T(8,128)(2,1)S(1)}, bf16[1,128,896]{2,1,0:T(8,128)(2,1)}, u32[]{:S(2)}) copy-start(bf16[1,128,896]{2,1,0:T(8,128)(2,1)} %param.9) | copy-start | bytes 688132
  100.3 13.3 %copy-start.4 = (s32[1,128,8]{1,2,0:T(8,128)S(1)}, s32[1,128,8]{1,2,0:T(8,128)}, u32[]{:S(2)}) copy-start(s32[1,128,8]{1,2,0:T(8,128)} %param.12) | copy-start | bytes 12292
  100.3 64.1 %all-to-all-start.3 = ((bf16[32,8,3584]{2,1,0:T(8,128)(2,1)}), bf16[32,8,3584]{2,1,0:T(8,128)(2,1)}, u32[]{:S(2)}, u32[]{:S(2)}) async-start(bf16[32,8,3584]{2,1,0:T(8,128)(2,1)} %bitcast.106), calls=%async_computation.3 | async-start | bytes 3670016 | tf_op jit(solution)/shard_map/all_to_all | solution.py:76
  110.2 9.5 %collective-permute-start = (bf16[1,128,896]{2,1,0:T(8,128)(2,1)S(1)}, bf16[1,128,896]{2,1,0:T(8,128)(2,1)S(1)}, u32[]{:S(2)}, u32[]{:S(2)}) collective-permute-start(bf16[1,128,896]{2,1,0:T(8,128)(2,1)S(1)} %copy-done.6), channel_id=1, source_target_pairs={{0,128},{128,256},{256,384},{384,0},{1,129},{129,257},{257,385},{3... | collective-permute-start | bytes 688136 | tf_op jit(solution)/shard_map/ppermute | solution.py:14
  165.8 18.3 %copy-start.1 = (bf16[1,1,3584,1,128]{4,2,3,1,0:T(8,128)(2,1)S(1)}, bf16[1,1,3584,1,128]{4,2,3,1,0:T(8,128)(2,1)}, u32[]{:S(2)}) copy-start(bf16[1,1,3584,1,128]{4,2,3,1,0:T(8,128)(2,1)} %param.17) | copy-start | bytes 2752516
  165.8 83.3 %all-to-all-start = ((bf16[32,8,3584]{2,1,0:T(8,128)(2,1)}), bf16[32,8,3584]{2,1,0:T(8,128)(2,1)}, u32[]{:S(2)}, u32[]{:S(2)}) async-start(bf16[32,8,3584]{2,1,0:T(8,128)(2,1)} %bitcast.107), calls=%async_computation | async-start | bytes 3670016 | tf_op jit(solution)/shard_map/all_to_all | solution.py:74
  184.1 99.6 %reduce-scatter.9.cloned.1.call-start = ((), (), s32[]{:S(2)}) async-start(), calls=%async_computation.10 | async-start | bytes 2293760
  192.2 107.7 %reduce-scatter.7.cloned.1.call-start = ((), (), s32[]{:S(2)}) async-start(), calls=%async_computation.9 | async-start | bytes 2293760
  265.7 30.2 %all-to-all-start.6 = ((bf16[32,1,8]{2,1,0:T(2,128)(2,1)}), bf16[32,1,8]{2,1,0:T(2,128)(2,1)S(1)}, u32[]{:S(2)}, u32[]{:S(2)}) async-start(bf16[32,1,8]{2,1,0:T(2,128)(2,1)} %all_to_all.36), calls=%async_computation.6 | async-start | bytes 32768 | tf_op jit(solution)/shard_map/all_to_all | solution.py:101
  283.7 39.2 %copy-start.5 = (bf16[1,128,8]{1,2,0:T(8,128)(2,1)S(1)}, bf16[1,128,8]{1,2,0:T(8,128)(2,1)}, u32[]{:S(2)}) copy-start(bf16[1,128,8]{1,2,0:T(8,128)(2,1)} %param.14) | copy-start | bytes 6148
  283.7 39.6 %copy-start.3 = (s32[1,128,8]{1,2,0:T(8,128)S(1)}, s32[1,128,8]{1,2,0:T(8,128)}, u32[]{:S(2)}) copy-start(s32[1,128,8]{1,2,0:T(8,128)} %param.13) | copy-start | bytes 12292
  295.9 20.8 %all-to-all-start.5 = ((bf16[32,8,896]{2,1,0:T(8,128)(2,1)}), bf16[32,8,896]{2,1,0:T(8,128)(2,1)S(1)}, u32[]{:S(2)}, u32[]{:S(2)}) async-start(bf16[32,8,896]{2,1,0:T(8,128)(2,1)} %bitcast.28), calls=%async_computation.5 | async-start | bytes 917504 | tf_op jit(solution)/shard_map/all_to_all | solution.py:100
  316.8 24.0 %all-to-all-start.1 = ((bf16[32,8,896]{2,1,0:T(8,128)(2,1)}), bf16[32,8,896]{2,1,0:T(8,128)(2,1)S(1)}, u32[]{:S(2)}, u32[]{:S(2)}) async-start(bf16[32,8,896]{2,1,0:T(8,128)(2,1)} %bitcast.8), calls=%async_computation.1 | async-start | bytes 917504 | tf_op jit(solution)/shard_map/all_to_all | solution.py:99
Sparse Core Ops, SparseCore 0:
  192.3 52.5 reduce-scatter.8
  257.1 36.8 reduce-scatter.6
where the time goes:
time: 350 us; the launch traced here: 349 us
  blocking collectives  106 us (30%)
  waiting for transfers between devices  106 us (30%)
  starting transfers between devices  84.9 us (24%)
  local copies, waits for them, and re-layouts  17.5 us (5%)
  matrix products  16.9 us (5%)
  between operations  14.4 us (4%)
    all_to_all x1, waiting for transfers between devices, on_device(): lax.all_to_all(pick_rows(select_a, full_a), 'ep', split_axis=0, concat_ax...  56.9 us
    all_gather x1, blocking collectives, on_device(): lax.all_gather(b_grad, 'rep', axis=2, tiled=True)  48.8 us
    all_gather x1, blocking collectives, on_device(): lax.all_gather(input_a, 'rep', axis=2, tiled=True)  42.2 us
    all_to_all x1, starting transfers between devices, on_device(): lax.all_to_all(pick_rows(select_a, full_a), 'ep', split_axis=0, concat_ax...  18.2 us
    all_to_all x1, starting transfers between devices, on_device(): lax.all_to_all(half_dg, 'ep', split_axis=0, concat_axis=0, tiled=True)  17.9 us
    all_to_all x1, starting transfers between devices, on_device(): lax.all_to_all(slot_gate, 'ep', split_axis=0, concat_axis=0, tiled=True)  16 us
    all_to_all x1, waiting for transfers between devices, on_device(): lax.all_to_all(half_a, 'ep', split_axis=0, concat_axis=0, tiled=True)  15.5 us
    all_to_all x1, waiting for transfers between devices, on_device(): lax.all_to_all(half_dx, 'ep', split_axis=0, concat_axis=0, tiled=True)  14.9 us
  transfers between devices with their start and end apart: 10, of which 6 were waited for; matrix products, arithmetic and copies ran while one was open for 8% of the time, Pallas kernels for 0%

commit v1 on v0

v1 whole, which is shorter than its diff:
```python
import jax
import jax.numpy as jnp
from jax import lax
from jax.sharding import PartitionSpec as P

CAP = 8
F32 = jnp.float32
BF16 = jnp.bfloat16


def passed_along(value, axis, by):
    size = lax.axis_size(axis)
    return lax.ppermute(value, axis, [(i, (i + by) % size) for i in range(size)])


def core_swap(value):
    return lax.ppermute(value, "rep", [(i, i ^ 1) for i in range(4)])


def chip_swap(value):
    return lax.ppermute(value, "rep", [(i, i ^ 2) for i in range(4)])


def over_ep(value):
    return lax.all_to_all(value, "ep", split_axis=0, concat_axis=0, tiled=True)


def tables(routes, gates, experts):
    match = (routes[:, :, None] == jnp.arange(experts, dtype=jnp.int32)).astype(F32)
    hits = jnp.sum(match, axis=1)
    weight = jnp.sum(gates.astype(F32)[:, :, None] * match, axis=1)
    rows = routes.shape[0]
    lower = jnp.tril(jnp.ones((rows, rows), BF16), -1)
    before = jnp.dot(lower, hits.astype(BF16), preferred_element_type=F32)
    select = hits[:, :, None] * (before[:, :, None] == jnp.arange(CAP, dtype=F32)).astype(F32)
    return match, select, weight


def mm(x, w):
    return jnp.dot(x, w, preferred_element_type=F32)


def mt(x, w):
    return lax.dot_general(x, w, (((1,), (1,)), ((), ())), preferred_element_type=F32)


def twice(select):
    t, e, c = select.shape
    return jnp.broadcast_to(select[:, :, None, :], (t, e, 2, c)).reshape(t, e * 2 * c)


def pick(select, values):
    t, e, c = select.shape
    n = len(values)
    eye = jnp.eye(n, dtype=F32)
    full = select[None, :, :, None, None, :] * eye[:, None, None, None, :, None]
    full = jnp.broadcast_to(full, (n, t, e, 2, n, c)).reshape(n * t, e * 2 * n * c).astype(BF16)
    stacked = values[0] if n == 1 else jnp.concatenate(values, axis=0)
    out = lax.dot_general(full, stacked, (((0,), (0,)), ((), ())), preferred_element_type=F32)
    return out.astype(BF16).reshape(e * 2, n * c, -1)


def on_device(a_sent, b_input, b_grad, routes_a, routes_b, gates_a, gates_b, w_in, w_down):
    experts = lax.axis_size("ep") // 2
    sources = 2 * experts
    rep = lax.axis_index("rep")
    dl = a_sent.shape[2]
    input_a = passed_along(a_sent, "pipe", 1)[0]

    match_b, select_b, weight_b = tables(routes_b[0], gates_b[0], experts)
    match_a, select_a, weight_a = tables(routes_a[0], gates_a[0], experts)

    got_bg = over_ep(pick(select_b, [b_input[0], b_grad[0]]))

    wi, wd = w_in[0, 0, :, 0, :], w_down[0, 0, :, 0, :]

    def part(w, index):
        return lax.dynamic_slice_in_dim(w, index * dl, dl, axis=0)

    wi_own, wi_oth = part(wi, rep), part(wi, rep ^ 1)
    wd_own, wd_oth = part(wd, rep), part(wd, rep ^ 1)
    wi_peer = chip_swap(jnp.concatenate([part(wi, rep ^ 2), part(wi, rep ^ 3)], axis=0))
    wd_peer = chip_swap(jnp.concatenate([part(wd, rep ^ 2), part(wd, rep ^ 3)], axis=0))
    wi_pown, wi_poth = wi_peer[:dl], wi_peer[dl:]
    wd_pown, wd_poth = wd_peer[:dl], wd_peer[dl:]

    got_a = over_ep(pick(select_a, [input_a]))

    oth_bg = core_swap(got_bg)
    xo, go = got_bg[:, :CAP].reshape(-1, dl), got_bg[:, CAP:].reshape(-1, dl)
    xt, gt = oth_bg[:, :CAP].reshape(-1, dl), oth_bg[:, CAP:].reshape(-1, dl)
    units = wd.shape[1]
    to_peer = jnp.concatenate(
        [mm(xo, wi_pown) + mm(xt, wi_poth), mm(go, wd_pown) + mm(gt, wd_poth)], axis=1
    ).astype(BF16)
    from_peer = chip_swap(to_peer).astype(F32)
    gu = mm(xo, wi_own) + mm(xt, wi_oth) + from_peer[:, : 2 * units]
    dh = mm(go, wd_own) + mm(gt, wd_oth) + from_peer[:, 2 * units :]
    g, u = gu[:, :units], gu[:, units:]
    sq = jax.nn.sigmoid(g)
    hid = (g * sq * u).astype(BF16)
    dg_part = jnp.sum(hid.astype(F32) * dh, axis=1).astype(BF16)
    d_gate = (dh * u * sq * (1.0 + g * (1.0 - sq))).astype(BF16)
    d_up = (dh * g * sq).astype(BF16)
    dgu = jnp.concatenate([d_gate, d_up], axis=1)
    pad = jnp.broadcast_to(dg_part[:, None], (dg_part.shape[0], 128))
    peer_dgu = chip_swap(jnp.concatenate([dgu, pad], axis=1))
    dg_chip = (pad.astype(F32) + peer_dgu[:, 2 * units :].astype(F32)).astype(BF16)
    dgp = peer_dgu[:, : 2 * units]
    dx_oth = (mt(dgu, wi_oth) + mt(dgp, wi_poth)).astype(BF16)
    dx_got = core_swap(jnp.concatenate([dx_oth, dg_chip], axis=1))
    dx_own = mt(dgu, wi_own) + mt(dgp, wi_pown) + dx_got[:, :dl].astype(F32)
    dg_all = dg_chip.astype(F32) + dx_got[:, dl:].astype(F32)
    back_b = over_ep(
        jnp.concatenate([dx_own, dg_all], axis=1).astype(BF16).reshape(sources, CAP, -1)
    )

    oth_a = core_swap(got_a)
    ao, at = got_a.reshape(-1, dl), oth_a.reshape(-1, dl)
    ga_peer = chip_swap((mm(ao, wi_pown) + mm(at, wi_poth)).astype(BF16))
    gu_a = mm(ao, wi_own) + mm(at, wi_oth) + ga_peer.astype(F32)
    hid_a = (jax.nn.silu(gu_a[:, :units]) * gu_a[:, units:]).astype(BF16)
    hid_p = chip_swap(hid_a)
    o_oth = core_swap((mt(hid_a, wd_oth) + mt(hid_p, wd_poth)).astype(BF16))
    o_own = mt(hid_a, wd_own) + mt(hid_p, wd_pown) + o_oth.astype(F32)
    back_a = over_ep(o_own.astype(BF16).reshape(sources, CAP, dl))

    dx = mm(twice(select_b * weight_b[:, :, None]).astype(BF16), back_b[:, :, :dl].reshape(-1, dl))
    dgs = back_b[:, :, dl].astype(F32).reshape(experts, 2, CAP)
    dgs = dgs[:, 0] + dgs[:, 1]
    per_expert = jnp.sum(select_b * dgs[None], axis=2)
    dgate = jnp.sum(match_b * per_expert[:, None, :], axis=2)
    y = mm(twice(select_a * weight_a[:, :, None]).astype(BF16), back_a.reshape(-1, dl))
    return y.astype(BF16)[None], dx.astype(BF16)[None], dgate.astype(BF16)[None]


def solution(mesh):
    rows = P("pipe", "ep", "rep")
    small = P("pipe", "ep", None)
    weights = P("pipe", "ep", None, "rep", None)
    return jax.shard_map(
        on_device,
        mesh=mesh,
        in_specs=(rows, rows, rows, small, small, small, small, weights, weights),
        out_specs=(rows, rows, small),
        check_vma=False,
    )
```

time: 350 us -> 195 us (0.56)
  the two profiles are of different devices: /device:TPU:2 before, /device:TPU:8 now
where the time goes in v1:
time: 195 us; the launch traced here: 194 us
  waiting for transfers between devices  93.5 us (48%)
  starting transfers between devices  66.7 us (34%)
  matrix products  23.4 us (12%)
  other arithmetic  8.48 us (4%)
    all_to_all x4, waiting for transfers between devices, over_ep(): return lax.all_to_all(value, 'ep', split_axis=0, concat_axis=0, tiled=True)  48.6 us
    ppermute x6, waiting for transfers between devices, chip_swap(): return lax.ppermute(value, 'rep', [(i, i ^ 2) for i in range(4)])  40.8 us
    all_to_all x4, starting transfers between devices, over_ep(): return lax.all_to_all(value, 'ep', split_axis=0, concat_axis=0, tiled=True)  38 us
    ppermute x6, starting transfers between devices, chip_swap(): return lax.ppermute(value, 'rep', [(i, i ^ 2) for i in range(4)])  17.4 us
    dot_general x14, matrix products, mm(): return jnp.dot(x, w, preferred_element_type=F32)  13.3 us
    ppermute x4, starting transfers between devices, core_swap(): return lax.ppermute(value, 'rep', [(i, i ^ 1) for i in range(4)])  7.8 us
    dot_general x8, matrix products, mt(): lax.dot_general(x, w, (((1,), (1,)), ((), ())), preferred_element_type=F32)  6.23 us
    ppermute x1, waiting for transfers between devices, passed_along(): lax.ppermute(value, axis, [(i, (i + by) % size) for i in range(size)])  4.08 us
  transfers between devices with their start and end apart: 15, of which 8 were waited for; matrix products, arithmetic and copies ran while one was open for 15% of the time, Pallas kernels for 0%

profile of v1, /device:TPU:8, one launch (start us, length us, event | category | flops | bytes accessed | tf_op | source)
XLA Modules:
  0.0 193.8 jit_solution(14299165235220054974)
XLA Ops:
  0.6 3.5 %collective-permute-start = (bf16[1,128,896]{2,1,0:T(8,128)(2,1)}, bf16[1,128,896]{2,1,0:T(8,128)(2,1)S(1)}, u32[]{:S(2)}, u32[]{:S(2)}) collective-permute-start(bf16[1,128,896]{2,1,0:T(8,128)(2,1)} %param.9), channel_id=1, source_target_pairs={{0,128},{128,256},{256,384},{384,0},{1,129},{129,257},{257,385},{3... | collective-permute-start | bytes 688136 | tf_op jit(solution)/shard_map/ppermute | solution.py:13
  7.3 4.1 %collective-permute-done = bf16[1,128,896]{2,1,0:T(8,128)(2,1)S(1)} collective-permute-done((bf16[1,128,896]{2,1,0:T(8,128)(2,1)}, bf16[1,128,896]{2,1,0:T(8,128)(2,1)S(1)}, u32[]{:S(2)}, u32[]{:S(2)}) %collective-permute-start) | collective-permute-done | bytes 229408 | tf_op jit(solution)/shard_map/ppermute | solution.py:13
  12.5 15.2 %all-to-all-start = ((bf16[32,8,896]{2,1,0:T(8,128)(2,1)}), bf16[32,8,896]{2,1,0:T(8,128)(2,1)S(1)}, u32[]{:S(2)}, u32[]{:S(2)}) async-start(bf16[32,8,896]{2,1,0:T(8,128)(2,1)} %fusion.7), calls=%async_computation | async-start | bytes 917504 | tf_op jit(solution)/shard_map/all_to_all | solution.py:25
  28.2 2.4 %convolution_convert_fusion = bf16[512,896]{1,0:T(8,128)(2,1)} fusion(bf16[128,896]{1,0:T(8,128)(2,1)S(1)} %bitcast.120, bf16[128,896]{1,0:T(8,128)(2,1)} %bitcast.121, bf16[64,8,2,128]{3,2,1,0:T(2,128)(2,1)S(1)} %bitcast.116), kind=kOutput, calls=%fused_computation | convolution fusion | flops 236257280 | bytes 1638400 | tf_op jit(solution)/shard_map/dot_general | solution.py:59
  30.6 12.9 %all-to-all-done = bf16[32,8,896]{2,1,0:T(8,128)(2,1)S(1)} async-done(((bf16[32,8,896]{2,1,0:T(8,128)(2,1)}), bf16[32,8,896]{2,1,0:T(8,128)(2,1)S(1)}, u32[]{:S(2)}, u32[]{:S(2)}) %all-to-all-start) | async-done | bytes 458784 | tf_op jit(solution)/shard_map/all_to_all | solution.py:25
  43.4 6.3 %all-to-all-start.2 = ((bf16[32,16,896]{2,1,0:T(8,128)(2,1)}), bf16[32,16,896]{2,1,0:T(8,128)(2,1)}, u32[]{:S(2)}, u32[]{:S(2)}) async-start(bf16[32,16,896]{2,1,0:T(8,128)(2,1)} %bitcast.24), calls=%async_computation.2 | async-start | bytes 1835008 | tf_op jit(solution)/shard_map/all_to_all | solution.py:25
  50.8 4.4 %collective-permute-start.2 = (bf16[1792,256]{1,0:T(8,128)(2,1)}, bf16[1792,256]{1,0:T(8,128)(2,1)S(1)}, u32[]{:S(2)}, u32[]{:S(2)}) collective-permute-start(bf16[1792,256]{1,0:T(8,128)(2,1)} %pad_maximum_fusion), channel_id=1, source_target_pairs={{0,64},{32,96},{64,0},{96,32},{1,65},{33,97},{65,1},{97,33},{2,66}... | collective-permute-start | bytes 2752520 | tf_op jit(solution)/shard_map/ppermute | solution.py:21
  55.2 1.9 collective-permute-start.1
  58.0 1.9 collective-permute-start.5
  59.9 33.2 %collective-permute-done.2 = bf16[1792,256]{1,0:T(8,128)(2,1)S(1)} collective-permute-done((bf16[1792,256]{1,0:T(8,128)(2,1)}, bf16[1792,256]{1,0:T(8,128)(2,1)S(1)}, u32[]{:S(2)}, u32[]{:S(2)}) %collective-permute-start.2) | collective-permute-done | bytes 917536 | tf_op jit(solution)/shard_map/ppermute | solution.py:21
  95.4 1.9 collective-permute-start.3
  97.7 2.1 %collective-permute-start.7 = (bf16[32,16,896]{2,1,0:T(8,128)(2,1)}, bf16[32,16,896]{2,1,0:T(8,128)(2,1)S(1)}, u32[]{:S(2)}, u32[]{:S(2)}) collective-permute-start(bf16[32,16,896]{2,1,0:T(8,128)(2,1)} %all-to-all-done.2), channel_id=1, source_target_pairs={{0,32},{32,0},{64,96},{96,64},{1,33},{33,1},{65,97},{97,65},{2,34}... | collective-permute-start | bytes 2752520 | tf_op jit(solution)/shard_map/ppermute | solution.py:17
  99.7 4.1 %collective-permute-done.3 = bf16[256,256]{1,0:T(8,128)(2,1)} collective-permute-done((bf16[256,256]{1,0:T(8,128)(2,1)}, bf16[256,256]{1,0:T(8,128)(2,1)}, u32[]{:S(2)}, u32[]{:S(2)}) %collective-permute-start.3) | collective-permute-done | bytes 131104 | tf_op jit(solution)/shard_map/ppermute | solution.py:21
  105.2 2.4 %collective-permute-start.4 = (bf16[256,128]{1,0:T(8,128)(2,1)S(1)}, bf16[256,128]{1,0:T(8,128)(2,1)S(1)}, u32[]{:S(2)}, u32[]{:S(2)}) collective-permute-start(bf16[256,128]{1,0:T(8,128)(2,1)S(1)} %fusion.68), channel_id=1, source_target_pairs={{0,64},{32,96},{64,0},{96,32},{1,65},{33,97},{65,1},{97,33},{2,66}... | collective-permute-start | bytes 196616 | tf_op jit(solution)/shard_map/ppermute | solution.py:21
  113.6 3.4 %collective-permute-start.8 = (bf16[256,384]{1,0:T(8,128)(2,1)S(1)}, bf16[256,384]{1,0:T(8,128)(2,1)S(1)}, u32[]{:S(2)}, u32[]{:S(2)}) collective-permute-start(bf16[256,384]{1,0:T(8,128)(2,1)S(1)} %pad_maximum_fusion.4), channel_id=1, source_target_pairs={{0,64},{32,96},{64,0},{96,32},{1,65},{33,97},{65,1},{97,33},{2,66}... | collective-permute-start | bytes 589832 | tf_op jit(solution)/shard_map/ppermute | solution.py:21
  118.3 2.8 %collective-permute-done.8 = bf16[256,384]{1,0:T(8,128)(2,1)S(1)} collective-permute-done((bf16[256,384]{1,0:T(8,128)(2,1)S(1)}, bf16[256,384]{1,0:T(8,128)(2,1)S(1)}, u32[]{:S(2)}, u32[]{:S(2)}) %collective-permute-start.8) | collective-permute-done | bytes 196640 | tf_op jit(solution)/shard_map/ppermute | solution.py:21
  122.1 3.4 %collective-permute-start.9 = (bf16[256,384]{1,0:T(8,128)(2,1)S(1)}, bf16[256,384]{1,0:T(8,128)(2,1)S(1)}, u32[]{:S(2)}, u32[]{:S(2)}) collective-permute-start(bf16[256,384]{1,0:T(8,128)(2,1)S(1)} %pad_maximum_fusion.5), channel_id=1, source_target_pairs={{0,64},{32,96},{64,0},{96,32},{1,65},{33,97},{65,1},{97,33},{2,66}... | collective-permute-start | bytes 589832 | tf_op jit(solution)/shard_map/ppermute | solution.py:21
  126.7 1.9 collective-permute-start.6
  130.9 1.9 collective-permute-start.10
  133.2 2.0 %fusion.6 = bf16[32,8,896]{2,1,0:T(8,128)(2,1)} fusion(f32[256,896]{1,0:T(8,128)S(1)} %fusion.57, bf16[256,128]{1,0:T(8,128)(2,1)S(1)} %collective-permute-done.4, bf16[256,896]{1,0:T(8,128)(2,1)S(1)} %collective-permute-done.6, bf16[1792,128]{1,0:T(8,128)(2,1)} %collective-permute-done.5), kind=kOutput, calls=%fused_computation.12 | convolution fusion | flops 59637760 | bytes 2129920 | tf_op jit(solution)/shard_map/dot_general | solution.py:44
  135.2 12.0 %all-to-all-start.1 = ((bf16[32,8,896]{2,1,0:T(8,128)(2,1)}), bf16[32,8,896]{2,1,0:T(8,128)(2,1)S(1)}, u32[]{:S(2)}, u32[]{:S(2)}) async-start(bf16[32,8,896]{2,1,0:T(8,128)(2,1)} %fusion.6), calls=%async_computation.1 | async-start | bytes 917504 | tf_op jit(solution)/shard_map/all_to_all | solution.py:25
  150.8 16.4 %all-to-all-done.1 = bf16[32,8,896]{2,1,0:T(8,128)(2,1)S(1)} async-done(((bf16[32,8,896]{2,1,0:T(8,128)(2,1)}), bf16[32,8,896]{2,1,0:T(8,128)(2,1)S(1)}, u32[]{:S(2)}, u32[]{:S(2)}) %all-to-all-start.1) | async-done | bytes 458784 | tf_op jit(solution)/shard_map/all_to_all | solution.py:25
  167.2 4.4 %all-to-all-start.3 = ((bf16[32,8,1024]{2,1,0:T(8,128)(2,1)}), bf16[32,8,1024]{2,1,0:T(8,128)(2,1)S(1)}, u32[]{:S(2)}, u32[]{:S(2)}) async-start(bf16[32,8,1024]{2,1,0:T(8,128)(2,1)} %pad_maximum_fusion.2), calls=%async_computation.3 | async-start | bytes 1048576 | tf_op jit(solution)/shard_map/all_to_all | solution.py:25
  172.7 19.3 %all-to-all-done.3 = bf16[32,8,1024]{2,1,0:T(8,128)(2,1)S(1)} async-done(((bf16[32,8,1024]{2,1,0:T(8,128)(2,1)}), bf16[32,8,1024]{2,1,0:T(8,128)(2,1)S(1)}, u32[]{:S(2)}, u32[]{:S(2)}) %all-to-all-start.3) | async-done | bytes 524320 | tf_op jit(solution)/shard_map/all_to_all | solution.py:25
  (91 shorter events, 28.6 us)
Async XLA Ops:
  0.6 27.1 %copy-start = (bf16[1,1,3584,1,256]{4,2,3,1,0:T(8,128)(2,1)S(1)}, bf16[1,1,3584,1,256]{4,2,3,1,0:T(8,128)(2,1)}, u32[]{:S(2)}) copy-start(bf16[1,1,3584,1,256]{4,2,3,1,0:T(8,128)(2,1)} %param.16) | copy-start | bytes 5505028
  0.6 10.8 %collective-permute-start = (bf16[1,128,896]{2,1,0:T(8,128)(2,1)}, bf16[1,128,896]{2,1,0:T(8,128)(2,1)S(1)}, u32[]{:S(2)}, u32[]{:S(2)}) collective-permute-start(bf16[1,128,896]{2,1,0:T(8,128)(2,1)} %param.9), channel_id=1, source_target_pairs={{0,128},{128,256},{256,384},{384,0},{1,129},{129,257},{257,385},{3... | collective-permute-start | bytes 688136 | tf_op jit(solution)/shard_map/ppermute | solution.py:13
  12.5 15.7 %copy-start.3 = (bf16[1,128,896]{2,1,0:T(8,128)(2,1)S(1)}, bf16[1,128,896]{2,1,0:T(8,128)(2,1)}, u32[]{:S(2)}) copy-start(bf16[1,128,896]{2,1,0:T(8,128)(2,1)} %param.11) | copy-start | bytes 688132
  12.5 30.9 %all-to-all-start = ((bf16[32,8,896]{2,1,0:T(8,128)(2,1)}), bf16[32,8,896]{2,1,0:T(8,128)(2,1)S(1)}, u32[]{:S(2)}, u32[]{:S(2)}) async-start(bf16[32,8,896]{2,1,0:T(8,128)(2,1)} %fusion.7), calls=%async_computation | async-start | bytes 917504 | tf_op jit(solution)/shard_map/all_to_all | solution.py:25
  43.4 54.2 %all-to-all-start.2 = ((bf16[32,16,896]{2,1,0:T(8,128)(2,1)}), bf16[32,16,896]{2,1,0:T(8,128)(2,1)}, u32[]{:S(2)}, u32[]{:S(2)}) async-start(bf16[32,16,896]{2,1,0:T(8,128)(2,1)} %bitcast.24), calls=%async_computation.2 | async-start | bytes 1835008 | tf_op jit(solution)/shard_map/all_to_all | solution.py:25
  49.8 7.3 %copy-start.1 = (bf16[1,1,3584,1,128]{4,2,3,1,0:T(8,128)(2,1)S(1)}, bf16[1,1,3584,1,128]{4,2,3,1,0:T(8,128)(2,1)}, u32[]{:S(2)}) copy-start(bf16[1,1,3584,1,128]{4,2,3,1,0:T(8,128)(2,1)} %param.17) | copy-start | bytes 2752516
  50.8 42.3 %collective-permute-start.2 = (bf16[1792,256]{1,0:T(8,128)(2,1)}, bf16[1792,256]{1,0:T(8,128)(2,1)S(1)}, u32[]{:S(2)}, u32[]{:S(2)}) collective-permute-start(bf16[1792,256]{1,0:T(8,128)(2,1)} %pad_maximum_fusion), channel_id=1, source_target_pairs={{0,64},{32,96},{64,0},{96,32},{1,65},{33,97},{65,1},{97,33},{2,66}... | collective-permute-start | bytes 2752520 | tf_op jit(solution)/shard_map/ppermute | solution.py:21
  55.2 38.0 %collective-permute-start.1 = (bf16[32,8,896]{2,1,0:T(8,128)(2,1)S(1)}, bf16[32,8,896]{2,1,0:T(8,128)(2,1)}, u32[]{:S(2)}, u32[]{:S(2)}) collective-permute-start(bf16[32,8,896]{2,1,0:T(8,128)(2,1)S(1)} %all-to-all-done), channel_id=1, source_target_pairs={{0,32},{32,0},{64,96},{96,64},{1,33},{33,1},{65,97},{97,65},{2,34}... | collective-permute-start | bytes 1376264 | tf_op jit(solution)/shard_map/ppermute | solution.py:17
  58.0 51.7 %collective-permute-start.5 = (bf16[1792,128]{1,0:T(8,128)(2,1)}, bf16[1792,128]{1,0:T(8,128)(2,1)}, u32[]{:S(2)}, u32[]{:S(2)}) collective-permute-start(bf16[1792,128]{1,0:T(8,128)(2,1)} %pad_maximum_fusion.3), channel_id=1, source_target_pairs={{0,64},{32,96},{64,0},{96,32},{1,65},{33,97},{65,1},{97,33},{2,66}... | collective-permute-start | bytes 1376264 | tf_op jit(solution)/shard_map/ppermute | solution.py:21
  95.4 8.4 %collective-permute-start.3 = (bf16[256,256]{1,0:T(8,128)(2,1)}, bf16[256,256]{1,0:T(8,128)(2,1)}, u32[]{:S(2)}, u32[]{:S(2)}) collective-permute-start(bf16[256,256]{1,0:T(8,128)(2,1)} %fusion.13), channel_id=1, source_target_pairs={{0,64},{32,96},{64,0},{96,32},{1,65},{33,97},{65,1},{97,33},{2,66}... | collective-permute-start | bytes 393224 | tf_op jit(solution)/shard_map/ppermute | solution.py:21
  97.7 10.0 %copy-start.2 = (bf16[1,1,3584,1,128]{4,2,3,1,0:T(8,128)(2,1)S(1)}, bf16[1,1,3584,1,128]{4,2,3,1,0:T(8,128)(2,1)}, u32[]{:S(2)}) copy-start(bf16[1,1,3584,1,128]{4,2,3,1,0:T(8,128)(2,1)} %param.17) | copy-start | bytes 2752516
  97.7 11.6 %collective-permute-start.7 = (bf16[32,16,896]{2,1,0:T(8,128)(2,1)}, bf16[32,16,896]{2,1,0:T(8,128)(2,1)S(1)}, u32[]{:S(2)}, u32[]{:S(2)}) collective-permute-start(bf16[32,16,896]{2,1,0:T(8,128)(2,1)} %all-to-all-done.2), channel_id=1, source_target_pairs={{0,32},{32,0},{64,96},{96,64},{1,33},{33,1},{65,97},{97,65},{2,34}... | collective-permute-start | bytes 2752520 | tf_op jit(solution)/shard_map/ppermute | solution.py:17
  105.2 20.2 %collective-permute-start.4 = (bf16[256,128]{1,0:T(8,128)(2,1)S(1)}, bf16[256,128]{1,0:T(8,128)(2,1)S(1)}, u32[]{:S(2)}, u32[]{:S(2)}) collective-permute-start(bf16[256,128]{1,0:T(8,128)(2,1)S(1)} %fusion.68), channel_id=1, source_target_pairs={{0,64},{32,96},{64,0},{96,32},{1,65},{33,97},{65,1},{97,33},{2,66}... | collective-permute-start | bytes 196616 | tf_op jit(solution)/shard_map/ppermute | solution.py:21
  113.6 7.6 %collective-permute-start.8 = (bf16[256,384]{1,0:T(8,128)(2,1)S(1)}, bf16[256,384]{1,0:T(8,128)(2,1)S(1)}, u32[]{:S(2)}, u32[]{:S(2)}) collective-permute-start(bf16[256,384]{1,0:T(8,128)(2,1)S(1)} %pad_maximum_fusion.4), channel_id=1, source_target_pairs={{0,64},{32,96},{64,0},{96,32},{1,65},{33,97},{65,1},{97,33},{2,66}... | collective-permute-start | bytes 589832 | tf_op jit(solution)/shard_map/ppermute | solution.py:21
  122.1 7.6 %collective-permute-start.9 = (bf16[256,384]{1,0:T(8,128)(2,1)S(1)}, bf16[256,384]{1,0:T(8,128)(2,1)S(1)}, u32[]{:S(2)}, u32[]{:S(2)}) collective-permute-start(bf16[256,384]{1,0:T(8,128)(2,1)S(1)} %pad_maximum_fusion.5), channel_id=1, source_target_pairs={{0,64},{32,96},{64,0},{96,32},{1,65},{33,97},{65,1},{97,33},{2,66}... | collective-permute-start | bytes 589832 | tf_op jit(solution)/shard_map/ppermute | solution.py:21
  126.7 6.4 %collective-permute-start.6 = (bf16[256,896]{1,0:T(8,128)(2,1)S(1)}, bf16[256,896]{1,0:T(8,128)(2,1)S(1)}, u32[]{:S(2)}, u32[]{:S(2)}) collective-permute-start(bf16[256,896]{1,0:T(8,128)(2,1)S(1)} %fusion.2), channel_id=1, source_target_pairs={{0,32},{32,0},{64,96},{96,64},{1,33},{33,1},{65,97},{97,65},{2,34}... | collective-permute-start | bytes 1376264 | tf_op jit(solution)/shard_map/ppermute | solution.py:17
  130.9 16.7 %collective-permute-start.10 = (bf16[256,1024]{1,0:T(8,128)(2,1)}, bf16[256,1024]{1,0:T(8,128)(2,1)}, u32[]{:S(2)}, u32[]{:S(2)}) collective-permute-start(bf16[256,1024]{1,0:T(8,128)(2,1)} %pad_maximum_fusion.1), channel_id=1, source_target_pairs={{0,32},{32,0},{64,96},{96,64},{1,33},{33,1},{65,97},{97,65},{2,34}... | collective-permute-start | bytes 1572872 | tf_op jit(solution)/shard_map/ppermute | solution.py:17
  135.2 32.0 %all-to-all-start.1 = ((bf16[32,8,896]{2,1,0:T(8,128)(2,1)}), bf16[32,8,896]{2,1,0:T(8,128)(2,1)S(1)}, u32[]{:S(2)}, u32[]{:S(2)}) async-start(bf16[32,8,896]{2,1,0:T(8,128)(2,1)} %fusion.6), calls=%async_computation.1 | async-start | bytes 917504 | tf_op jit(solution)/shard_map/all_to_all | solution.py:25
  147.6 24.0 %copy-start.12 = (bf16[1,128,8]{1,2,0:T(8,128)(2,1)S(1)}, bf16[1,128,8]{1,2,0:T(8,128)(2,1)}, u32[]{:S(2)}) copy-start(bf16[1,128,8]{1,2,0:T(8,128)(2,1)} %param.15) | copy-start | bytes 6148
  147.6 24.1 %copy-start.5 = (f32[128,16]{0,1:T(8,128)S(1)}, f32[128,16]{0,1:T(8,128)}, u32[]{:S(2)}) copy-start(f32[128,16]{0,1:T(8,128)} %copy-done.4) | copy-start | bytes 24580
  147.6 24.1 %copy-start.6 = (f32[128,16]{0,1:T(8,128)S(1)}, f32[128,16]{0,1:T(8,128)}, u32[]{:S(2)}) copy-start(f32[128,16]{0,1:T(8,128)} %get-tuple-element.6) | copy-start | bytes 24580
  147.6 24.1 %copy-start.8 = (f32[128,16]{0,1:T(8,128)S(1)}, f32[128,16]{0,1:T(8,128)}, u32[]{:S(2)}) copy-start(f32[128,16]{0,1:T(8,128)} %copy-done.7) | copy-start | bytes 24580
  149.0 43.2 %copy-start.9 = (s32[1,128,8]{1,2,0:T(8,128)S(1)}, s32[1,128,8]{1,2,0:T(8,128)}, u32[]{:S(2)}) copy-start(s32[1,128,8]{1,2,0:T(8,128)} %param.13) | copy-start | bytes 12292
  167.2 24.8 %all-to-all-start.3 = ((bf16[32,8,1024]{2,1,0:T(8,128)(2,1)}), bf16[32,8,1024]{2,1,0:T(8,128)(2,1)S(1)}, u32[]{:S(2)}, u32[]{:S(2)}) async-start(bf16[32,8,1024]{2,1,0:T(8,128)(2,1)} %pad_maximum_fusion.2), calls=%async_computation.3 | async-start | bytes 1048576 | tf_op jit(solution)/shard_map/all_to_all | solution.py:25
  (4 other events, 13.0 us)

commit v2 on v1

v2 whole, which is shorter than its diff:
```python
import jax
import jax.numpy as jnp
from jax import lax
from jax.experimental import pallas as pl
from jax.experimental.pallas import tpu as pltpu
from jax.sharding import Mesh
from jax.sharding import PartitionSpec as P

CAP = 8
NY = 4
F32 = jnp.float32
BF16 = jnp.bfloat16
VMEM = pl.BlockSpec(memory_space=pltpu.VMEM)


def call(kernel, outs, args, flops):
    moved = sum(x.size * x.dtype.itemsize for x in (*args, *outs))
    return pl.pallas_call(
        kernel,
        out_shape=outs,
        in_specs=[VMEM] * len(args),
        out_specs=[VMEM] * len(outs),
        compiler_params=pltpu.CompilerParams(vmem_limit_bytes=24 << 20),
        cost_estimate=pl.CostEstimate(flops=flops, bytes_accessed=moved, transcendentals=0),
    )(*args)


def like(shape, dtype=BF16):
    return jax.ShapeDtypeStruct(shape, dtype)


def ring(axis, by):
    size = lax.axis_size(axis)
    return [(i, (i + by) % size) for i in range(size)]


def core_swap(value):
    return lax.ppermute(value, "rep", [(i, i ^ 1) for i in range(4)])


def chip_swap(value):
    return lax.ppermute(value, "rep", [(i, i ^ 2) for i in range(4)])


def mm(x, w):
    return jnp.dot(x, w, preferred_element_type=F32)


def mt(x, w):
    return lax.dot_general(x, w, (((1,), (1,)), ((), ())), preferred_element_type=F32)


def lanes_of(width):
    return lax.broadcasted_iota(jnp.int32, (1, width), 1)


def slot_table(routes, gates, width, per_expert):
    rows = routes.shape[0]
    lane = lanes_of(width)
    expert = lane // per_expert
    hit = jnp.zeros((rows, width), F32)
    weight = jnp.zeros((rows, width), F32)
    for k in range(routes.shape[1]):
        named = routes[:, k : k + 1] == expert
        hit = jnp.where(named, 1.0, hit)
        weight = jnp.where(named, gates[:, k : k + 1], weight)
    row = lax.broadcasted_iota(jnp.int32, (rows, rows), 0)
    col = lax.broadcasted_iota(jnp.int32, (rows, rows), 1)
    lower = jnp.where(col < row, 1.0, 0.0).astype(BF16)
    before = mm(lower, hit.astype(BF16))
    select = jnp.where(before == (lane % CAP).astype(F32), hit, 0.0)
    return select, weight * select


def tables_kernel(ra, rb, ga, gb, sel_a, sel_b, sel2_b, wt_a, wt_b):
    slots = sel_a.shape[1]
    for r, g, sel, sel2, wt in ((ra, ga, sel_a, None, wt_a), (rb, gb, sel_b, sel2_b, wt_b)):
        routes, gates = r[...], g[...].astype(F32)
        sel[...] = slot_table(routes, gates, slots, CAP)[0].astype(BF16)
        two, weight = slot_table(routes, gates, 2 * slots, 2 * CAP)
        wt[...] = weight.astype(BF16)
        if sel2 is not None:
            sel2[...] = two.astype(BF16)


def pick_kernel(sel_a, sel_b, a, b, g, out):
    def picked(sel, x):
        return lax.dot_general(
            sel[...], x[...], (((0,), (0,)), ((), ())), preferred_element_type=F32
        )

    parts = [picked(sel_a, a), picked(sel_b, b), picked(sel_b, g)]
    for z in range(out.shape[0]):
        rows = [
            p[(2 * z + m) * CAP : (2 * z + m + 1) * CAP] for m in range(2) for p in parts
        ]
        out[z] = jnp.concatenate(rows, axis=0).astype(BF16)


def features_kernel(index, wi, wd, out):
    units = wd.shape[1]
    out[:, : 2 * units] = wi[...]
    out[:, 2 * units :] = wd[...]


def spread_kernel(z_rows, out):
    nz = z_rows.shape[0]
    wide = [z_rows[z].astype(F32) for z in range(nz)]
    for m in range(2):
        rows = [
            wide[z][(3 * m + q) * CAP : (3 * m + q + 1) * CAP] for q in range(3) for z in range(nz)
        ]
        both = jnp.concatenate(rows, axis=0).astype(BF16)
        out[2 * m] = both
        out[2 * m + 1] = both


def first_a_kernel(own, oth, w, out):
    dl, units2 = own.shape[2], out.shape[2]
    n = out.shape[1]
    for s in range(NY):
        x = mm(own[s, :n], w[:dl, :units2]) + mm(oth[s, :n], w[dl:, :units2])
        out[s] = x.astype(out.dtype)


def first_b_kernel(own, oth, w, out):
    dl = own.shape[2]
    n, units = out.shape[1], out.shape[2] // 3
    for s in range(NY):
        x, g = slice(n, 2 * n), slice(2 * n, 3 * n)
        gu = mm(own[s, x], w[:dl, : 2 * units]) + mm(oth[s, x], w[dl:, : 2 * units])
        dh = mm(own[s, g], w[:dl, 2 * units :]) + mm(oth[s, g], w[dl:, 2 * units :])
        out[s, :, : 2 * units] = gu.astype(out.dtype)
        out[s, :, 2 * units :] = dh.astype(out.dtype)


def by_source(value):
    nz = value.shape[0] // (NY * CAP)
    rows = [
        value[(s * nz + z) * CAP : (s * nz + z + 1) * CAP] for z in range(nz) for s in range(NY)
    ]
    return jnp.concatenate(rows, axis=0)


def middle_a_kernel(self_ref, peer_ref, out):
    units = out.shape[1]
    v = self_ref[...] + peer_ref[...].astype(F32)
    g, u = v[:, :units], v[:, units:]
    out[...] = by_source(g * jax.nn.sigmoid(g) * u).astype(BF16)


def middle_b_kernel(self_ref, peer_ref, out):
    units = out.shape[1] // 3
    v = self_ref[...] + peer_ref[...].astype(F32)
    g, u, dh = v[:, :units], v[:, units : 2 * units], v[:, 2 * units :]
    sq = jax.nn.sigmoid(g)
    hid = (g * sq * u).astype(BF16).astype(F32)
    dgate = jnp.broadcast_to(jnp.sum(hid * dh, axis=1, keepdims=True), g.shape)
    d_gate = dh * u * sq * (1.0 + g * (1.0 - sq))
    d_up = dh * g * sq
    out[...] = by_source(jnp.concatenate([d_gate, d_up, dgate], axis=1)).astype(BF16)


def last_a_kernel(mine, peer, w_self, w_peer, out):
    units = mine.shape[1]
    o = mt(mine[...], w_self[:, 2 * units :]) + mt(peer[...], w_peer[:, 2 * units :])
    out[...] = o.astype(out.dtype)


def last_b_kernel(mine, peer, w_self, w_peer, out):
    dl = w_self.shape[0]
    units = mine.shape[1] // 3
    m, p = mine[...], peer[...]
    dx = mt(m[:, : 2 * units], w_self[:, : 2 * units]) + mt(
        p[:, : 2 * units], w_peer[:, : 2 * units]
    )
    out[:, :dl] = dx.astype(out.dtype)
    dg = (m[:, 2 * units :].astype(F32) + p[:, 2 * units :].astype(F32)).astype(BF16)
    out[:, dl:] = dg.astype(out.dtype)


def add_kernel(kept_a, core_a, kept_b, core_b, out):
    dl = kept_a.shape[1]
    out[:, :dl] = (kept_a[...] + core_a[...].astype(F32)).astype(BF16)
    out[:, dl:] = (kept_b[...] + core_b[...].astype(F32)).astype(BF16)


def combine_kernel(back, wt_a, wt_b, sel2_b, routes, y, dx, dgate):
    dl = y.shape[1]
    y[...] = mm(wt_a[...], back[:, :dl]).astype(BF16)
    dx[...] = mm(wt_b[...], back[:, dl : 2 * dl]).astype(BF16)
    dg = back[:, 2 * dl :]
    expert = lanes_of(sel2_b.shape[1]) // (2 * CAP)
    sel = sel2_b[...].astype(F32)
    topk = dgate.shape[1]
    out = jnp.zeros((sel.shape[0], dg.shape[1]), F32)
    lane = lanes_of(dg.shape[1])
    for k in range(topk):
        chosen = jnp.where(routes[:, k : k + 1] == expert, sel, 0.0).astype(BF16)
        out = jnp.where(lane == k, mm(chosen, dg), out)
    dgate[...] = out[:, :topk].astype(BF16)


def on_device(a_sent, b_input, b_grad, routes_a, routes_b, gates_a, gates_b, w_in, w_down):
    nz = lax.axis_size("z")
    sources, experts = nz * NY, nz * 2
    slots = experts * CAP
    rep = lax.axis_index("rep")
    tok, dl = a_sent.shape[1:]
    wi, wd = w_in[0, 0, :, 0, :], w_down[0, 0, :, 0, :]
    units = wd.shape[1]
    n = nz * CAP

    input_a = lax.ppermute(a_sent, "pipe", ring("pipe", 1))

    def features(*index):
        parts = len(index)
        return pl.pallas_call(
            features_kernel,
            out_shape=like((parts * dl, 3 * units)),
            grid_spec=pltpu.PrefetchScalarGridSpec(
                num_scalar_prefetch=1,
                grid=(parts,),
                in_specs=[
                    pl.BlockSpec((dl, 2 * units), lambda i, index: (index[i], 0)),
                    pl.BlockSpec((dl, units), lambda i, index: (index[i], 0)),
                ],
                out_specs=pl.BlockSpec((dl, 3 * units), lambda i, index: (i, 0)),
            ),
            compiler_params=pltpu.CompilerParams(vmem_limit_bytes=24 << 20),
            cost_estimate=pl.CostEstimate(
                flops=0, bytes_accessed=12 * parts * dl * units, transcendentals=0
            ),
        )(jnp.stack(index).astype(jnp.int32), wi, wd)

    w_peer = chip_swap(features(rep ^ 2, rep ^ 3))
    ra, rb, ga, gb = routes_a[0], routes_b[0], gates_a[0], gates_b[0]
    sel_a, sel_b, sel2_b, wt_a, wt_b = call(
        tables_kernel,
        [like((tok, slots)), like((tok, slots))] + [like((tok, 2 * slots))] * 3,
        [ra, rb, ga, gb],
        6 * tok * tok * slots * 2,
    )
    z_out = call(
        pick_kernel,
        [like((nz, 6 * CAP, dl))],
        [sel_a, sel_b, input_a[0], b_input[0], b_grad[0]],
        6 * tok * slots * dl,
    )[0]
    z_all = lax.all_to_all(z_out, "z", 0, 0, tiled=True)
    w_self = features(rep, rep ^ 1)
    z_all, w_peer, w_self = lax.optimization_barrier((z_all, w_peer, w_self))

    def one(kernel, shape, args, flops):
        return call(kernel, [shape], args, flops)[0]

    own = one(spread_kernel, like((NY, 3 * n, dl)), [z_all], NY * 3 * n * dl)
    own = lax.all_to_all(own, "yh", 0, 0, tiled=True)
    oth = core_swap(own)

    work = 2 * NY * n * 2 * dl * 2 * units
    peer_a = one(first_a_kernel, like((NY, n, 2 * units)), [own, oth, w_peer], work)
    peer_a = chip_swap(peer_a)
    peer_b = one(first_b_kernel, like((NY, n, 3 * units)), [own, oth, w_peer], work)
    peer_b = chip_swap(peer_b)
    self_a = one(first_a_kernel, like((NY, n, 2 * units), F32), [own, oth, w_self], work)
    self_b = one(first_b_kernel, like((NY, n, 3 * units), F32), [own, oth, w_self], work)

    rows = NY * n
    hid = one(
        middle_a_kernel,
        like((rows, units)),
        [self_a.reshape(rows, -1), peer_a.reshape(rows, -1)],
        work // 100,
    )
    hid_peer = chip_swap(hid)
    dgu = one(
        middle_b_kernel,
        like((rows, 3 * units)),
        [self_b.reshape(rows, -1), peer_b.reshape(rows, -1)],
        work // 100,
    )
    dgu_peer = chip_swap(dgu)
    args_a, args_b = [hid, hid_peer], [dgu, dgu_peer]
    w_own, w_oth = [w_self[:dl], w_peer[:dl]], [w_self[dl:], w_peer[dl:]]
    core_a = core_swap(one(last_a_kernel, like((rows, dl)), args_a + w_oth, work // 2))
    core_b = core_swap(one(last_b_kernel, like((rows, dl + units)), args_b + w_oth, work))
    kept_a = one(last_a_kernel, like((rows, dl), F32), args_a + w_own, work // 2)
    kept_b = one(last_b_kernel, like((rows, dl + units), F32), args_b + w_own, work)
    back = one(
        add_kernel, like((rows, 2 * dl + units)), [kept_a, core_a, kept_b, core_b], rows * dl
    )
    back = lax.all_to_all(back.reshape(sources, CAP, -1), ("z", "yh"), 0, 0, tiled=True)
    back = back.reshape(rows, -1)

    y, dx, dgate = call(
        combine_kernel,
        [like((tok, dl)), like((tok, dl)), like((tok, routes_b.shape[2]))],
        [back, wt_a, wt_b, sel2_b, rb],
        4 * tok * rows * dl,
    )
    return y[None], dx[None], dgate[None]


def solution(mesh):
    pipe, rep, ep = mesh.devices.shape
    split = Mesh(mesh.devices.reshape(pipe, rep, ep // NY, NY), ("pipe", "rep", "z", "yh"))
    rows = P("pipe", ("z", "yh"), "rep")
    small = P("pipe", ("z", "yh"), None)
    weights = P("pipe", ("z", "yh"), None, "rep", None)
    return jax.shard_map(
        on_device,
        mesh=split,
        in_specs=(rows, rows, rows, small, small, small, small, weights, weights),
        out_specs=(rows, rows, small),
        check_vma=False,
    )
```

time: 195 us -> 158 us (0.81)
  the two profiles are of different devices: /device:TPU:8 before, /device:TPU:2 now
where the time goes in v2:
time: 158 us; the launch traced here: 157 us
  blocking collectives  78 us (49%)
  starting transfers between devices  35.1 us (22%)
  waiting for transfers between devices  24 us (15%)
  Pallas kernels  11 us (7%)
  local copies, waits for them, and re-layouts  8.02 us (5%)
    all_to_all x1, blocking collectives, on_device(): own = lax.all_to_all(own, 'yh', 0, 0, tiled=True)  41.1 us
    all_to_all x1, blocking collectives, on_device(): lax.all_to_all(back.reshape(sources, CAP, -1), ('z', 'yh'), 0, 0, tiled=T...  36.9 us
    ppermute x5, waiting for transfers between devices, chip_swap(): return lax.ppermute(value, 'rep', [(i, i ^ 2) for i in range(4)])  16.2 us
    ppermute x5, starting transfers between devices, chip_swap(): return lax.ppermute(value, 'rep', [(i, i ^ 2) for i in range(4)])  15.1 us
    all_to_all x1, starting transfers between devices, on_device(): z_all = lax.all_to_all(z_out, 'z', 0, 0, tiled=True)  10.3 us
    pallas_call x15, Pallas kernels, call(): pl.pallas_call(kernel, out_shape=outs, in_specs=[VMEM] * len(args), out_s...  8.56 us
    unnamed x37, local copies, waits for them, and re-layouts  7.75 us
    ppermute x3, starting transfers between devices, core_swap(): return lax.ppermute(value, 'rep', [(i, i ^ 1) for i in range(4)])  6.25 us
  transfers between devices with their start and end apart: 10, of which 6 were waited for; matrix products, arithmetic and copies ran while one was open for 1% of the time, Pallas kernels for 6%

profile of v2, /device:TPU:2, one launch (start us, length us, event | category | flops | bytes accessed | tf_op | source)
XLA Modules:
  0.0 157.2 jit_solution(4676175157978598744)
XLA Ops:
  0.6 3.4 %collective-permute-start = (bf16[1,128,896]{2,1,0:T(8,128)(2,1)}, bf16[1,128,896]{2,1,0:T(8,128)(2,1)S(1)}, u32[]{:S(2)}, u32[]{:S(2)}) collective-permute-start(bf16[1,128,896]{2,1,0:T(8,128)(2,1)} %param.9), channel_id=1, source_target_pairs={{0,128},{128,256},{256,384},{384,0},{1,129},{129,257},{257,385},{3... | collective-permute-start | bytes 688136 | tf_op jit(solution)/shard_map/ppermute | solution.py:214
  4.1 1.5 copy-done
  5.6 1.2 copy-done.2
  6.8 1.7 %shard_map.114 = bf16[1792,384]{1,0:T(8,128)(2,1)} custom-call(s32[2]{0:T(128)S(1)} %pad_add_fusion.index, bf16[3584,256]{1,0:T(8,128)(2,1)S(1)} %bitcast.22, bf16[3584,128]{1,0:T(8,128)(2,1)S(1)} %bitcast.26), custom_call_target="tpu_custom_call" | custom-call | bytes 2752512 | tf_op jit(solution)/shard_map/pallas_call | solution.py:218
  8.6 3.5 %collective-permute-start.1 = (bf16[1792,384]{1,0:T(8,128)(2,1)}, bf16[1792,384]{1,0:T(8,128)(2,1)S(1)}, u32[]{:S(2)}, u32[]{:S(2)}) collective-permute-start(bf16[1792,384]{1,0:T(8,128)(2,1)} %shard_map.114), channel_id=1, source_target_pairs={{0,64},{32,96},{64,0},{96,32},{1,65},{33,97},{65,1},{97,33},{2,66}... | collective-permute-start | bytes 4128776 | tf_op jit(solution)/shard_map/ppermute | solution.py:42
  14.5 1.2 shard_map.113
  15.7 10.3 %all-to-all-start = ((bf16[8,48,896]{2,1,0:T(8,128)(2,1)}), bf16[8,48,896]{2,1,0:T(8,128)(2,1)S(1)}, u32[]{:S(2)}, u32[]{:S(2)}) async-start(bf16[8,48,896]{2,1,0:T(8,128)(2,1)} %shard_map.113), calls=%async_computation | async-start | bytes 1376256 | tf_op jit(solution)/shard_map/all_to_all | solution.py:250
  26.1 1.5 copy-done.1
  27.6 1.2 copy-done.3
  29.5 12.8 %collective-permute-done.1.w = bf16[1792,384]{1,0:T(8,128)(2,1)S(1)} collective-permute-done((bf16[1792,384]{1,0:T(8,128)(2,1)}, bf16[1792,384]{1,0:T(8,128)(2,1)S(1)}, u32[]{:S(2)}, u32[]{:S(2)}) %collective-permute-start.1) | collective-permute-done | bytes 1376288 | tf_op jit(solution)/shard_map/ppermute | solution.py:42
  42.3 4.2 %all-to-all-done.z_rows = bf16[8,48,896]{2,1,0:T(8,128)(2,1)S(1)} async-done(((bf16[8,48,896]{2,1,0:T(8,128)(2,1)}), bf16[8,48,896]{2,1,0:T(8,128)(2,1)S(1)}, u32[]{:S(2)}, u32[]{:S(2)}) %all-to-all-start) | async-done | bytes 688160 | tf_op jit(solution)/shard_map/all_to_all | solution.py:250
  46.6 41.1 %all_to_all.15.own = bf16[4,192,896]{2,1,0:T(8,128)(2,1)S(1)} all-to-all(bf16[4,192,896]{2,1,0:T(8,128)(2,1)S(1)} %shard_map.116), channel_id=1, replica_groups=mesh['pipe'=4,'rep'=4,'z'=8,'yh'=4] {'yh'}, dimensions={0} | all-to-all | bytes 2752512 | tf_op jit(solution)/shard_map/all_to_all | solution.py:258
  87.7 1.9 %collective-permute-start.2 = (bf16[4,192,896]{2,1,0:T(8,128)(2,1)S(1)}, bf16[4,192,896]{2,1,0:T(8,128)(2,1)S(1)}, u32[]{:S(2)}, u32[]{:S(2)}) collective-permute-start(bf16[4,192,896]{2,1,0:T(8,128)(2,1)S(1)} %all_to_all.15.own), channel_id=1, source_target_pairs={{0,32},{32,0},{64,96},{96,64},{1,33},{33,1},{65,97},{97,65},{2,34}... | collective-permute-start | bytes 4128776 | tf_op jit(solution)/shard_map/ppermute | solution.py:38
  89.6 3.1 %collective-permute-done.2.oth = bf16[4,192,896]{2,1,0:T(8,128)(2,1)S(1)} collective-permute-done((bf16[4,192,896]{2,1,0:T(8,128)(2,1)S(1)}, bf16[4,192,896]{2,1,0:T(8,128)(2,1)S(1)}, u32[]{:S(2)}, u32[]{:S(2)}) %collective-permute-start.2) | collective-permute-done | bytes 1376288 | tf_op jit(solution)/shard_map/ppermute | solution.py:38
  93.6 2.6 %collective-permute-start.6 = (bf16[4,64,384]{2,1,0:T(8,128)(2,1)S(1)}, bf16[4,64,384]{2,1,0:T(8,128)(2,1)S(1)}, u32[]{:S(2)}, u32[]{:S(2)}) collective-permute-start(bf16[4,64,384]{2,1,0:T(8,128)(2,1)S(1)} %shard_map.123), channel_id=1, source_target_pairs={{0,64},{32,96},{64,0},{96,32},{1,65},{33,97},{65,1},{97,33},{2,66}... | collective-permute-start | bytes 589832 | tf_op jit(solution)/shard_map/ppermute | solution.py:42
  97.0 3.2 %collective-permute-start.3 = (bf16[4,64,256]{2,1,0:T(8,128)(2,1)S(1)}, bf16[4,64,256]{2,1,0:T(8,128)(2,1)S(1)}, u32[]{:S(2)}, u32[]{:S(2)}) collective-permute-start(bf16[4,64,256]{2,1,0:T(8,128)(2,1)S(1)} %shard_map.118), channel_id=1, source_target_pairs={{0,64},{32,96},{64,0},{96,32},{1,65},{33,97},{65,1},{97,33},{2,66}... | collective-permute-start | bytes 393224 | tf_op jit(solution)/shard_map/ppermute | solution.py:42
  101.2 2.1 %collective-permute-done.6 = bf16[4,64,384]{2,1,0:T(8,128)(2,1)S(1)} collective-permute-done((bf16[4,64,384]{2,1,0:T(8,128)(2,1)S(1)}, bf16[4,64,384]{2,1,0:T(8,128)(2,1)S(1)}, u32[]{:S(2)}, u32[]{:S(2)}) %collective-permute-start.6) | collective-permute-done | bytes 196640 | tf_op jit(solution)/shard_map/ppermute | solution.py:42
  103.4 2.3 %collective-permute-start.7 = (bf16[256,384]{1,0:T(8,128)(2,1)S(1)}, bf16[256,384]{1,0:T(8,128)(2,1)S(1)}, u32[]{:S(2)}, u32[]{:S(2)}) collective-permute-start(bf16[256,384]{1,0:T(8,128)(2,1)S(1)} %shard_map.124.mine), channel_id=1, source_target_pairs={{0,64},{32,96},{64,0},{96,32},{1,65},{33,97},{65,1},{97,33},{2,66}... | collective-permute-start | bytes 589832 | tf_op jit(solution)/shard_map/ppermute | solution.py:42
  106.8 3.5 %collective-permute-start.4 = (bf16[256,128]{1,0:T(8,128)(2,1)S(1)}, bf16[256,128]{1,0:T(8,128)(2,1)S(1)}, u32[]{:S(2)}, u32[]{:S(2)}) collective-permute-start(bf16[256,128]{1,0:T(8,128)(2,1)S(1)} %shard_map.119.mine), channel_id=1, source_target_pairs={{0,64},{32,96},{64,0},{96,32},{1,65},{33,97},{65,1},{97,33},{2,66}... | collective-permute-start | bytes 196616 | tf_op jit(solution)/shard_map/ppermute | solution.py:42
  110.4 1.3 collective-permute-done.7.peer
  112.2 1.9 %collective-permute-start.8 = (bf16[256,1024]{1,0:T(8,128)(2,1)S(1)}, bf16[256,1024]{1,0:T(8,128)(2,1)S(1)}, u32[]{:S(2)}, u32[]{:S(2)}) collective-permute-start(bf16[256,1024]{1,0:T(8,128)(2,1)S(1)} %shard_map.126), channel_id=1, source_target_pairs={{0,32},{32,0},{64,96},{96,64},{1,33},{33,1},{65,97},{97,65},{2,34}... | collective-permute-start | bytes 1572872 | tf_op jit(solution)/shard_map/ppermute | solution.py:38
  114.5 2.4 %collective-permute-start.5 = (bf16[256,896]{1,0:T(8,128)(2,1)S(1)}, bf16[256,896]{1,0:T(8,128)(2,1)S(1)}, u32[]{:S(2)}, u32[]{:S(2)}) collective-permute-start(bf16[256,896]{1,0:T(8,128)(2,1)S(1)} %shard_map.121), channel_id=1, source_target_pairs={{0,32},{32,0},{64,96},{96,64},{1,33},{33,1},{65,97},{97,65},{2,34}... | collective-permute-start | bytes 1376264 | tf_op jit(solution)/shard_map/ppermute | solution.py:38
  118.6 36.9 %all_to_all.16 = bf16[32,8,1920]{2,1,0:T(8,128)(2,1)S(1)} all-to-all(bf16[32,8,1920]{2,1,0:T(8,128)(2,1)S(1)} %bitcast.25), channel_id=1, replica_groups=mesh['pipe'=4,'rep'=4,'z'=8,'yh'=4] {'z','yh'}, dimensions={0} | all-to-all | bytes 1966080 | tf_op jit(solution)/shard_map/all_to_all | solution.py:293
  155.5 1.1 shard_map.128
  (55 shorter events, 10.4 us)
Async XLA Ops:
  0.6 13.8 %collective-permute-start = (bf16[1,128,896]{2,1,0:T(8,128)(2,1)}, bf16[1,128,896]{2,1,0:T(8,128)(2,1)S(1)}, u32[]{:S(2)}, u32[]{:S(2)}) collective-permute-start(bf16[1,128,896]{2,1,0:T(8,128)(2,1)} %param.9), channel_id=1, source_target_pairs={{0,128},{128,256},{256,384},{384,0},{1,129},{129,257},{257,385},{3... | collective-permute-start | bytes 688136 | tf_op jit(solution)/shard_map/ppermute | solution.py:214
  4.1 1.5 copy-start
  5.6 1.2 copy-start.2
  6.8 5.3 %copy-start.14 = (bf16[1,128,8]{1,2,0:T(8,128)(2,1)S(1)}, bf16[1,128,8]{1,2,0:T(8,128)(2,1)}, u32[]{:S(2)}) copy-start(bf16[1,128,8]{1,2,0:T(8,128)(2,1)} %param.14) | copy-start | bytes 6148
  6.8 5.4 %copy-start.15 = (bf16[1,128,8]{1,2,0:T(8,128)(2,1)S(1)}, bf16[1,128,8]{1,2,0:T(8,128)(2,1)}, u32[]{:S(2)}) copy-start(bf16[1,128,8]{1,2,0:T(8,128)(2,1)} %param.15) | copy-start | bytes 6148
  6.8 5.5 %copy-start.12 = (s32[1,128,8]{1,2,0:T(8,128)S(1)}, s32[1,128,8]{1,2,0:T(8,128)}, u32[]{:S(2)}) copy-start(s32[1,128,8]{1,2,0:T(8,128)} %param.12) | copy-start | bytes 12292
  6.8 5.6 %copy-start.13 = (s32[1,128,8]{1,2,0:T(8,128)S(1)}, s32[1,128,8]{1,2,0:T(8,128)}, u32[]{:S(2)}) copy-start(s32[1,128,8]{1,2,0:T(8,128)} %param.13) | copy-start | bytes 12292
  6.8 7.7 %copy-start.4 = (bf16[1,128,896]{2,1,0:T(8,128)(2,1)S(1)}, bf16[1,128,896]{2,1,0:T(8,128)(2,1)}, u32[]{:S(2)}) copy-start(bf16[1,128,896]{2,1,0:T(8,128)(2,1)} %param.10) | copy-start | bytes 688132
  6.8 7.7 %copy-start.5 = (bf16[1,128,896]{2,1,0:T(8,128)(2,1)S(1)}, bf16[1,128,896]{2,1,0:T(8,128)(2,1)}, u32[]{:S(2)}) copy-start(bf16[1,128,896]{2,1,0:T(8,128)(2,1)} %param.11) | copy-start | bytes 688132
  8.6 33.7 %collective-permute-start.1 = (bf16[1792,384]{1,0:T(8,128)(2,1)}, bf16[1792,384]{1,0:T(8,128)(2,1)S(1)}, u32[]{:S(2)}, u32[]{:S(2)}) collective-permute-start(bf16[1792,384]{1,0:T(8,128)(2,1)} %shard_map.114), channel_id=1, source_target_pairs={{0,64},{32,96},{64,0},{96,32},{1,65},{33,97},{65,1},{97,33},{2,66}... | collective-permute-start | bytes 4128776 | tf_op jit(solution)/shard_map/ppermute | solution.py:42
  14.5 1.2 copy-start.10
  15.7 30.8 %all-to-all-start = ((bf16[8,48,896]{2,1,0:T(8,128)(2,1)}), bf16[8,48,896]{2,1,0:T(8,128)(2,1)S(1)}, u32[]{:S(2)}, u32[]{:S(2)}) async-start(bf16[8,48,896]{2,1,0:T(8,128)(2,1)} %shard_map.113), calls=%async_computation | async-start | bytes 1376256 | tf_op jit(solution)/shard_map/all_to_all | solution.py:250
  26.1 1.5 copy-start.1
  27.6 1.2 copy-start.3
  87.7 5.0 %collective-permute-start.2 = (bf16[4,192,896]{2,1,0:T(8,128)(2,1)S(1)}, bf16[4,192,896]{2,1,0:T(8,128)(2,1)S(1)}, u32[]{:S(2)}, u32[]{:S(2)}) collective-permute-start(bf16[4,192,896]{2,1,0:T(8,128)(2,1)S(1)} %all_to_all.15.own), channel_id=1, source_target_pairs={{0,32},{32,0},{64,96},{96,64},{1,33},{33,1},{65,97},{97,65},{2,34}... | collective-permute-start | bytes 4128776 | tf_op jit(solution)/shard_map/ppermute | solution.py:38
  93.6 9.6 %collective-permute-start.6 = (bf16[4,64,384]{2,1,0:T(8,128)(2,1)S(1)}, bf16[4,64,384]{2,1,0:T(8,128)(2,1)S(1)}, u32[]{:S(2)}, u32[]{:S(2)}) collective-permute-start(bf16[4,64,384]{2,1,0:T(8,128)(2,1)S(1)} %shard_map.123), channel_id=1, source_target_pairs={{0,64},{32,96},{64,0},{96,32},{1,65},{33,97},{65,1},{97,33},{2,66}... | collective-permute-start | bytes 589832 | tf_op jit(solution)/shard_map/ppermute | solution.py:42
  97.0 9.7 %collective-permute-start.3 = (bf16[4,64,256]{2,1,0:T(8,128)(2,1)S(1)}, bf16[4,64,256]{2,1,0:T(8,128)(2,1)S(1)}, u32[]{:S(2)}, u32[]{:S(2)}) collective-permute-start(bf16[4,64,256]{2,1,0:T(8,128)(2,1)S(1)} %shard_map.118), channel_id=1, source_target_pairs={{0,64},{32,96},{64,0},{96,32},{1,65},{33,97},{65,1},{97,33},{2,66}... | collective-permute-start | bytes 393224 | tf_op jit(solution)/shard_map/ppermute | solution.py:42
  103.4 8.3 %collective-permute-start.7 = (bf16[256,384]{1,0:T(8,128)(2,1)S(1)}, bf16[256,384]{1,0:T(8,128)(2,1)S(1)}, u32[]{:S(2)}, u32[]{:S(2)}) collective-permute-start(bf16[256,384]{1,0:T(8,128)(2,1)S(1)} %shard_map.124.mine), channel_id=1, source_target_pairs={{0,64},{32,96},{64,0},{96,32},{1,65},{33,97},{65,1},{97,33},{2,66}... | collective-permute-start | bytes 589832 | tf_op jit(solution)/shard_map/ppermute | solution.py:42
  106.8 7.2 %collective-permute-start.4 = (bf16[256,128]{1,0:T(8,128)(2,1)S(1)}, bf16[256,128]{1,0:T(8,128)(2,1)S(1)}, u32[]{:S(2)}, u32[]{:S(2)}) collective-permute-start(bf16[256,128]{1,0:T(8,128)(2,1)S(1)} %shard_map.119.mine), channel_id=1, source_target_pairs={{0,64},{32,96},{64,0},{96,32},{1,65},{33,97},{65,1},{97,33},{2,66}... | collective-permute-start | bytes 196616 | tf_op jit(solution)/shard_map/ppermute | solution.py:42
  112.2 6.2 %collective-permute-start.8 = (bf16[256,1024]{1,0:T(8,128)(2,1)S(1)}, bf16[256,1024]{1,0:T(8,128)(2,1)S(1)}, u32[]{:S(2)}, u32[]{:S(2)}) collective-permute-start(bf16[256,1024]{1,0:T(8,128)(2,1)S(1)} %shard_map.126), channel_id=1, source_target_pairs={{0,32},{32,0},{64,96},{96,64},{1,33},{33,1},{65,97},{97,65},{2,34}... | collective-permute-start | bytes 1572872 | tf_op jit(solution)/shard_map/ppermute | solution.py:38
  114.5 3.8 %collective-permute-start.5 = (bf16[256,896]{1,0:T(8,128)(2,1)S(1)}, bf16[256,896]{1,0:T(8,128)(2,1)S(1)}, u32[]{:S(2)}, u32[]{:S(2)}) collective-permute-start(bf16[256,896]{1,0:T(8,128)(2,1)S(1)} %shard_map.121), channel_id=1, source_target_pairs={{0,32},{32,0},{64,96},{96,64},{1,33},{33,1},{65,97},{97,65},{2,34}... | collective-permute-start | bytes 1376264 | tf_op jit(solution)/shard_map/ppermute | solution.py:38
  118.5 36.9 %copy-start.7 = (bf16[128,256]{1,0:T(8,128)(2,1)S(1)}, bf16[128,256]{1,0:T(8,128)(2,1)}, u32[]{:S(2)}) copy-start(bf16[128,256]{1,0:T(8,128)(2,1)} %copy-done.6) | copy-start | bytes 196612
  118.5 36.9 %copy-start.9 = (bf16[128,256]{1,0:T(8,128)(2,1)S(1)}, bf16[128,256]{1,0:T(8,128)(2,1)}, u32[]{:S(2)}) copy-start(bf16[128,256]{1,0:T(8,128)(2,1)} %copy-done.8) | copy-start | bytes 196612
  118.6 36.9 %copy-start.11 = (bf16[128,256]{1,0:T(8,128)(2,1)S(1)}, bf16[128,256]{1,0:T(8,128)(2,1)}, u32[]{:S(2)}) copy-start(bf16[128,256]{1,0:T(8,128)(2,1)} %copy-done.10) | copy-start | bytes 196612
  (2 other events, 1.2 us)

commit v3 on v2

v3 whole, which is shorter than its diff:
```python
import jax
import jax.numpy as jnp
from jax import lax
from jax.experimental import pallas as pl
from jax.experimental.pallas import tpu as pltpu
from jax.sharding import Mesh
from jax.sharding import PartitionSpec as P

CAP = 8
NY = 4
PAD = 16
F32 = jnp.float32
BF16 = jnp.bfloat16
VMEM = pl.BlockSpec(memory_space=pltpu.VMEM)
SMEM = pl.BlockSpec(memory_space=pltpu.SMEM)
HBM = pl.BlockSpec(memory_space=pl.ANY)


def call(kernel, outs, args, flops, specs=None):
    moved = sum(x.size * x.dtype.itemsize for x in (*args, *outs))
    return pl.pallas_call(
        kernel,
        out_shape=outs,
        in_specs=specs or [VMEM] * len(args),
        out_specs=[VMEM] * len(outs),
        compiler_params=pltpu.CompilerParams(vmem_limit_bytes=24 << 20),
        cost_estimate=pl.CostEstimate(flops=flops, bytes_accessed=moved, transcendentals=0),
    )(*args)


def like(shape, dtype=BF16):
    return jax.ShapeDtypeStruct(shape, dtype)


def ring(axis, by):
    size = lax.axis_size(axis)
    return [(i, (i + by) % size) for i in range(size)]


def core_swap(value):
    return lax.ppermute(value, "rep", [(i, i ^ 1) for i in range(4)])


def chip_swap(value):
    return lax.ppermute(value, "rep", [(i, i ^ 2) for i in range(4)])


def diag_swap(value):
    return lax.ppermute(value, "rep", [(i, i ^ 3) for i in range(4)])


def mm(x, w):
    return jnp.dot(x, w, preferred_element_type=F32)


def mt(x, w):
    return lax.dot_general(x, w, (((1,), (1,)), ((), ())), preferred_element_type=F32)


def lanes_of(width):
    return lax.broadcasted_iota(jnp.int32, (1, width), 1)


def slot_table(routes, gates, width, per_expert):
    rows = routes.shape[0]
    lane = lanes_of(width)
    expert = (lane // per_expert).astype(F32)
    hit = jnp.zeros((rows, width), F32)
    weight = jnp.zeros((rows, width), F32)
    for k in range(routes.shape[1]):
        named = routes[:, k : k + 1] == expert
        hit = jnp.where(named, 1.0, hit)
        if gates is not None:
            weight = jnp.where(named, gates[:, k : k + 1], weight)
    row = lax.broadcasted_iota(jnp.int32, (rows, rows), 0)
    col = lax.broadcasted_iota(jnp.int32, (rows, rows), 1)
    lower = jnp.where(col < row, 1.0, 0.0).astype(BF16)
    before = mm(lower, hit.astype(BF16))
    select = jnp.where(before == (lane % CAP).astype(F32), hit, 0.0)
    return select, weight * select


def column(value):
    return value[...].astype(F32).T


def tables_kernel(ra, rb, sel_a, sel_b):
    for r, sel in ((ra, sel_a), (rb, sel_b)):
        sel[...] = slot_table(column(r), None, sel.shape[1], CAP)[0].astype(BF16)


def weights_kernel(ra, rb, ga, gb, sel_b, wt_a, wt_b):
    for r, g, sel, wt in ((ra, ga, None, wt_a), (rb, gb, sel_b, wt_b)):
        select, weight = slot_table(column(r), column(g), wt.shape[1], 2 * CAP)
        wt[...] = weight.astype(BF16)
        if sel is not None:
            sel[...] = select.astype(BF16)


def picked(sel, x):
    return lax.dot_general(sel[...], x[...], (((0,), (0,)), ((), ())), preferred_element_type=F32)


def pick_b_kernel(sel_b, b, g, rows_b, rows_g):
    rows_b[...] = picked(sel_b, b)
    rows_g[...] = picked(sel_b, g)


def pick_kernel(sel_a, a, rows_b, rows_g, out):
    parts = [picked(sel_a, a), rows_b[...], rows_g[...]]
    for z in range(out.shape[0]):
        rows = [
            p[(2 * z + m) * CAP : (2 * z + m + 1) * CAP] for m in range(2) for p in parts
        ]
        out[z] = jnp.concatenate(rows, axis=0).astype(BF16)


def features_kernel(index, wi, wd, out, sems):
    count, dl, _ = out.shape
    units = wd.shape[1]
    copies = []
    for i in range(count):
        rows = pl.ds(pl.multiple_of(index[i] * dl, dl), dl)
        to = out.at[i]
        copies.append(pltpu.make_async_copy(wi.at[rows], to.at[:, : 2 * units], sems.at[2 * i]))
        copies.append(pltpu.make_async_copy(wd.at[rows], to.at[:, 2 * units :], sems.at[2 * i + 1]))
    for copy in copies:
        copy.start()
    for copy in copies:
        copy.wait()


def gather_kernel(rep, mine, core, chip, diag, out):
    r = rep[0]
    for step, w in enumerate((mine, core, chip, diag)):
        out[r ^ step] = w[...]


def spread_kernel(z_rows, out):
    nz = z_rows.shape[0]
    wide = [z_rows[z].astype(F32) for z in range(nz)]
    for m in range(2):
        rows = [
            wide[z][(3 * m + q) * CAP : (3 * m + q + 1) * CAP] for q in range(3) for z in range(nz)
        ]
        both = jnp.concatenate(rows, axis=0).astype(BF16)
        out[2 * m] = both
        out[2 * m + 1] = both


def first_kernel(index, own, w, out):
    units = w.shape[2] // 3
    n = own.shape[1] // 3
    for i in range(2):
        at = 5 * units * i
        wi, wd = w[index[i], :, : 2 * units], w[index[i], :, 2 * units :]
        for s in range(NY):
            gu = mm(own[s, : 2 * n], wi).astype(out.dtype)
            rows = slice(s * n, (s + 1) * n)
            out[rows, at : at + 2 * units] = gu[:n]
            out[rows, at + 2 * units : at + 4 * units] = gu[n:]
            out[rows, at + 4 * units : at + 5 * units] = mm(own[s, 2 * n :], wd).astype(out.dtype)


def add_kernel(kept, core, out):
    wide = out.shape[1]
    out[...] = (kept[:, wide:] + core[:, wide:].astype(F32)).astype(BF16)


def by_source(value):
    nz = value.shape[0] // (NY * CAP)
    rows = [
        value[(s * nz + z) * CAP : (s * nz + z + 1) * CAP] for z in range(nz) for s in range(NY)
    ]
    return jnp.concatenate(rows, axis=0)


def middle_kernel(kept, core, chip, out):
    wide = chip.shape[1]
    units = out.shape[1] // 3
    rows = kept.shape[0]
    v = kept[:, :wide] + core[:, :wide].astype(F32) + chip[...].astype(F32)
    ag, au, g, u, dh = [v[:, i * units : (i + 1) * units] for i in range(5)]
    hid_a = ag * jax.nn.sigmoid(ag) * au
    sq = jax.nn.sigmoid(g)
    hid = (g * sq * u).astype(BF16).astype(F32)
    dgate = jnp.broadcast_to(jnp.sum(hid * dh, axis=1, keepdims=True), g.shape)
    d_gate = dh * u * sq * (1.0 + g * (1.0 - sq))
    d_up = dh * g * sq
    out[:rows] = by_source(jnp.concatenate([hid_a, d_gate, d_up], axis=1)).astype(BF16)
    last = by_source(dgate).T[:PAD]
    fill = jnp.zeros((PAD, out.shape[1] - rows), F32)
    out[rows:] = jnp.concatenate([last, fill], axis=1).astype(BF16)


def last_kernel(hidden, w, out):
    blocks, dl, units = w.shape[0], w.shape[1], w.shape[2] // 3
    rows = out.shape[0]
    o = jnp.zeros((rows, dl), F32)
    dx = jnp.zeros((rows, dl), F32)
    dg = jnp.zeros((1, rows), F32)
    for j in range(blocks):
        o = o + mt(hidden[j, :rows, :units], w[j, :, 2 * units :])
        dx = dx + mt(hidden[j, :rows, units:], w[j, :, : 2 * units])
        dg = dg + hidden[j, rows:, :rows].astype(F32)[:1]
    out[:, :dl] = o.astype(BF16)
    out[:, dl : 2 * dl] = dx.astype(BF16)
    out[:, 2 * dl :] = jnp.broadcast_to(dg, (units, rows)).T.astype(BF16)


def combine_kernel(back, wt_a, wt_b, sel2_b, routes, y, dx, dgate):
    dl = y.shape[1]
    y[...] = mm(wt_a[...], back[:, :dl]).astype(BF16)
    dx[...] = mm(wt_b[...], back[:, dl : 2 * dl]).astype(BF16)
    dg = back[:, 2 * dl :]
    expert = (lanes_of(sel2_b.shape[1]) // (2 * CAP)).astype(F32)
    routes = column(routes)
    sel = sel2_b[...].astype(F32)
    topk = dgate.shape[0]
    out = jnp.zeros((sel.shape[0], dg.shape[1]), F32)
    lane = lanes_of(dg.shape[1])
    for k in range(topk):
        chosen = jnp.where(routes[:, k : k + 1] == expert, sel, 0.0).astype(BF16)
        out = jnp.where(lane == k, mm(chosen, dg), out)
    dgate[...] = out.T[:topk].astype(BF16)


def on_device(a_sent, b_input, b_grad, routes_a, routes_b, gates_a, gates_b, w_in, w_down):
    nz = lax.axis_size("z")
    sources, experts = nz * NY, nz * 2
    slots = experts * CAP
    rep = lax.axis_index("rep")
    tok, dl = a_sent.shape[1:]
    wi, wd = w_in[0, 0, :, 0, :], w_down[0, 0, :, 0, :]
    units = wd.shape[1]
    n = nz * CAP

    input_a = lax.ppermute(a_sent, "pipe", ring("pipe", 1))

    def features(*index):
        count = len(index)
        return pl.pallas_call(
            features_kernel,
            out_shape=like((count, dl, 3 * units)),
            in_specs=[SMEM, HBM, HBM],
            out_specs=HBM,
            scratch_shapes=[pltpu.SemaphoreType.DMA((2 * count,))],
            compiler_params=pltpu.CompilerParams(vmem_limit_bytes=24 << 20),
            cost_estimate=pl.CostEstimate(
                flops=0, bytes_accessed=12 * count * dl * units, transcendentals=0
            ),
        )(jnp.stack(index).astype(jnp.int32), wi, wd)

    def one(kernel, shape, args, flops, scalars=None):
        if scalars is None:
            return call(kernel, [shape], args, flops)[0]
        args = [jnp.stack(scalars).astype(jnp.int32), *args]
        return call(kernel, [shape], args, flops, [SMEM] + [VMEM] * (len(args) - 1))[0]

    w_chip = chip_swap(features(rep ^ 2, rep ^ 3))
    ra, rb, ga, gb = routes_a[0].T, routes_b[0].T, gates_a[0].T, gates_b[0].T
    sel_a, sel_b = call(
        tables_kernel, [like((tok, slots))] * 2, [ra, rb], 4 * tok * tok * slots
    )
    rows_b, rows_g = call(
        pick_b_kernel,
        [like((slots, dl), F32)] * 2,
        [sel_b, b_input[0], b_grad[0]],
        4 * tok * slots * dl,
    )
    z_out = one(
        pick_kernel,
        like((nz, 6 * CAP, dl)),
        [sel_a, input_a[0], rows_b, rows_g],
        2 * tok * slots * dl,
    )
    z_all = lax.all_to_all(z_out, "z", 0, 0, tiled=True)
    z_all, w_chip = lax.optimization_barrier((z_all, w_chip))
    w_here = features(rep, rep ^ 1)
    w_core = core_swap(w_here[1])
    w_diag = core_swap(w_chip[1])
    w_all = one(
        gather_kernel,
        like((4, dl, 3 * units)),
        [w_here[0], w_core, w_chip[0], w_diag],
        4 * dl * units,
        [rep],
    )

    own = one(spread_kernel, like((NY, 3 * n, dl)), [z_all], NY * 3 * n * dl)
    own = lax.all_to_all(own, "yh", 0, 0, tiled=True)

    rows, wide = NY * n, 5 * units
    work = 2 * rows * dl * 2 * wide
    core = one(first_kernel, like((rows, 2 * wide)), [own, w_all], work, [rep ^ 1, rep ^ 3])
    core = core_swap(core)
    kept = one(first_kernel, like((rows, 2 * wide), F32), [own, w_all], work, [rep, rep ^ 2])
    chip = chip_swap(one(add_kernel, like((rows, wide)), [kept, core], rows * wide))
    mine = one(middle_kernel, like((rows + PAD, 3 * units)), [kept, core, chip], rows * units * 40)
    hidden = lax.all_gather(mine, "rep")
    back = one(
        last_kernel, like((rows, 2 * dl + units)), [hidden, w_all], 2 * rows * dl * 12 * units
    )
    back, ra, rb, ga, gb = lax.optimization_barrier((back, ra, rb, ga, gb))
    back = lax.all_to_all(back.reshape(sources, CAP, -1), ("z", "yh"), 0, 0, tiled=True)
    back = back.reshape(rows, -1)

    sel_b, wt_a, wt_b = call(
        weights_kernel, [like((tok, 2 * slots))] * 3, [ra, rb, ga, gb], 8 * tok * tok * slots
    )
    y, dx, dgate = call(
        combine_kernel,
        [like((tok, dl)), like((tok, dl)), like((routes_b.shape[2], tok))],
        [back, wt_a, wt_b, sel_b, rb],
        4 * tok * rows * dl,
    )
    return y[None], dx[None], dgate.T[None]


def solution(mesh):
    pipe, rep, ep = mesh.devices.shape
    split = Mesh(mesh.devices.reshape(pipe, rep, ep // NY, NY), ("pipe", "rep", "z", "yh"))
    rows = P("pipe", ("z", "yh"), "rep")
    small = P("pipe", ("z", "yh"), None)
    weights = P("pipe", ("z", "yh"), None, "rep", None)
    return jax.shard_map(
        on_device,
        mesh=split,
        in_specs=(rows, rows, rows, small, small, small, small, weights, weights),
        out_specs=(rows, rows, small),
        check_vma=False,
    )
```

time: 158 us -> 156 us (0.987)
  the two profiles are of different devices: /device:TPU:2 before, /device:TPU:8 now
where the time goes in v3:
time: 156 us
  waiting for transfers between devices  86.4 us (55%)
  starting transfers between devices  41.3 us (26%)
  Pallas kernels  13.3 us (9%)
  blocking collectives  8.37 us (5%)
  local copies, waits for them, and re-layouts  5.26 us (3%)
    all_to_all x1, waiting for transfers between devices, on_device(): lax.all_to_all(back.reshape(sources, CAP, -1), ('z', 'yh'), 0, 0, tiled=T...  29.2 us
    ppermute x2, waiting for transfers between devices, chip_swap(): return lax.ppermute(value, 'rep', [(i, i ^ 2) for i in range(4)])  28.6 us
    all_to_all x1, waiting for transfers between devices, on_device(): own = lax.all_to_all(own, 'yh', 0, 0, tiled=True)  25.3 us
    pallas_call x12, Pallas kernels, call(): pl.pallas_call(kernel, out_shape=outs, in_specs=specs or [VMEM] * len(arg...  11.8 us
    all_to_all x1, starting transfers between devices, on_device(): lax.all_to_all(back.reshape(sources, CAP, -1), ('z', 'yh'), 0, 0, tiled=T...  9.36 us
    all_gather x1, blocking collectives, on_device(): hidden = lax.all_gather(mine, 'rep')  8.37 us
    ppermute x2, starting transfers between devices, chip_swap(): return lax.ppermute(value, 'rep', [(i, i ^ 2) for i in range(4)])  8.17 us
    all_to_all x1, starting transfers between devices, on_device(): own = lax.all_to_all(own, 'yh', 0, 0, tiled=True)  7.29 us
  transfers between devices with their start and end apart: 9, of which 6 were waited for; matrix products, arithmetic and copies ran while one was open for 1% of the time, Pallas kernels for 4%

profile of v3, /device:TPU:8, one launch (start us, length us, event | category | flops | bytes accessed | tf_op | source)
XLA Modules:
  0.0 155.8 jit_solution(17451024766982894511)
XLA Ops:
  0.6 3.4 %collective-permute-start = (bf16[1,128,896]{2,1,0:T(8,128)(2,1)}, bf16[1,128,896]{2,1,0:T(8,128)(2,1)S(1)}, u32[]{:S(2)}, u32[]{:S(2)}) collective-permute-start(bf16[1,128,896]{2,1,0:T(8,128)(2,1)} %param.9), channel_id=1, source_target_pairs={{0,128},{128,256},{256,384},{384,0},{1,129},{129,257},{257,385},{3... | collective-permute-start | bytes 688136 | tf_op jit(solution)/shard_map/ppermute | solution.py:238
  4.1 1.5 copy-done
  5.6 1.2 copy-done.3
  7.5 6.3 %collective-permute-start.1 = (bf16[2,896,384]{2,1,0:T(8,128)(2,1)S(1)}, bf16[2,896,384]{2,1,0:T(8,128)(2,1)}, u32[]{:S(2)}, u32[]{:S(2)}) collective-permute-start(bf16[2,896,384]{2,1,0:T(8,128)(2,1)S(1)} %shard_map.115), channel_id=1, source_target_pairs={{0,64},{32,96},{64,0},{96,32},{1,65},{33,97},{65,1},{97,33},{2,66}... | collective-permute-start | bytes 4128776 | tf_op jit(solution)/shard_map/ppermute | solution.py:45
  15.9 6.8 %all-to-all-start = ((bf16[8,48,896]{2,1,0:T(8,128)(2,1)}), bf16[8,48,896]{2,1,0:T(8,128)(2,1)S(1)}, u32[]{:S(2)}, u32[]{:S(2)}) async-start(bf16[8,48,896]{2,1,0:T(8,128)(2,1)} %shard_map.114), calls=%async_computation | async-start | bytes 1376256 | tf_op jit(solution)/shard_map/all_to_all | solution.py:277
  22.7 18.5 %collective-permute-done.1 = bf16[2,896,384]{2,1,0:T(8,128)(2,1)} collective-permute-done((bf16[2,896,384]{2,1,0:T(8,128)(2,1)S(1)}, bf16[2,896,384]{2,1,0:T(8,128)(2,1)}, u32[]{:S(2)}, u32[]{:S(2)}) %collective-permute-start.1) | collective-permute-done | bytes 1376288 | tf_op jit(solution)/shard_map/ppermute | solution.py:45
  41.2 1.6 %all-to-all-done.z_rows = bf16[8,48,896]{2,1,0:T(8,128)(2,1)S(1)} async-done(((bf16[8,48,896]{2,1,0:T(8,128)(2,1)}), bf16[8,48,896]{2,1,0:T(8,128)(2,1)S(1)}, u32[]{:S(2)}, u32[]{:S(2)}) %all-to-all-start) | async-done | bytes 688160 | tf_op jit(solution)/shard_map/all_to_all | solution.py:277
  42.8 1.2 shard_map.116
  44.0 7.3 %all-to-all-start.1 = ((bf16[4,192,896]{2,1,0:T(8,128)(2,1)}), bf16[4,192,896]{2,1,0:T(8,128)(2,1)}, u32[]{:S(2)}, u32[]{:S(2)}) async-start(bf16[4,192,896]{2,1,0:T(8,128)(2,1)} %shard_map.116), calls=%async_computation.1 | async-start | bytes 2752512 | tf_op jit(solution)/shard_map/all_to_all | solution.py:291
  52.3 1.9 %collective-permute-start.2 = (bf16[896,384]{1,0:T(8,128)(2,1)S(1)}, bf16[896,384]{1,0:T(8,128)(2,1)S(1)}, u32[]{:S(2)}, u32[]{:S(2)}) collective-permute-start(bf16[896,384]{1,0:T(8,128)(2,1)S(1)} %get-tuple-element.39), channel_id=1, source_target_pairs={{0,32},{32,0},{64,96},{96,64},{1,33},{33,1},{65,97},{97,65},{2,34}... | collective-permute-start | bytes 2064392 | tf_op jit(solution)/shard_map/ppermute | solution.py:41
  54.2 1.4 slice_bitcast_fusion.2
  55.7 2.4 %collective-permute-start.3 = (bf16[896,384]{1,0:T(8,128)(2,1)S(1)}, bf16[896,384]{1,0:T(8,128)(2,1)S(1)}, u32[]{:S(2)}, u32[]{:S(2)}) collective-permute-start(bf16[896,384]{1,0:T(8,128)(2,1)S(1)} %get-tuple-element.37), channel_id=1, source_target_pairs={{0,32},{32,0},{64,96},{96,64},{1,33},{33,1},{65,97},{97,65},{2,34}... | collective-permute-start | bytes 2064392 | tf_op jit(solution)/shard_map/ppermute | solution.py:41
  58.2 1.7 %collective-permute-done.3.diag = bf16[896,384]{1,0:T(8,128)(2,1)S(1)} collective-permute-done((bf16[896,384]{1,0:T(8,128)(2,1)S(1)}, bf16[896,384]{1,0:T(8,128)(2,1)S(1)}, u32[]{:S(2)}, u32[]{:S(2)}) %collective-permute-start.3) | collective-permute-done | bytes 688160 | tf_op jit(solution)/shard_map/ppermute | solution.py:41
  60.1 25.3 %all-to-all-done.1.own = bf16[4,192,896]{2,1,0:T(8,128)(2,1)} async-done(((bf16[4,192,896]{2,1,0:T(8,128)(2,1)}), bf16[4,192,896]{2,1,0:T(8,128)(2,1)}, u32[]{:S(2)}, u32[]{:S(2)}) %all-to-all-start.1) | async-done | bytes 1376288 | tf_op jit(solution)/shard_map/all_to_all | solution.py:291
  85.4 2.4 %shard_map.120 = bf16[256,1280]{1,0:T(8,128)(2,1)S(1)} custom-call(s32[2]{0:T(128)S(1)} %pad_add_fusion.3.index, bf16[4,192,896]{2,1,0:T(8,128)(2,1)} %all-to-all-done.1.own, bf16[4,896,384]{2,1,0:T(8,128)(2,1)S(1)} %shard_map.118.w), custom_call_target="tpu_custom_call" | custom-call | flops 587202560 | bytes 4784136 | tf_op jit(solution)/shard_map/pallas_call | solution.py:21
  87.8 1.9 %collective-permute-start.4 = (bf16[256,1280]{1,0:T(8,128)(2,1)S(1)}, bf16[256,1280]{1,0:T(8,128)(2,1)S(1)}, u32[]{:S(2)}, u32[]{:S(2)}) collective-permute-start(bf16[256,1280]{1,0:T(8,128)(2,1)S(1)} %shard_map.120), channel_id=1, source_target_pairs={{0,32},{32,0},{64,96},{96,64},{1,33},{33,1},{65,97},{97,65},{2,34}... | collective-permute-start | bytes 1966088 | tf_op jit(solution)/shard_map/ppermute | solution.py:41
  89.8 2.4 %shard_map.119.kept = f32[256,1280]{1,0:T(8,128)S(1)} custom-call(s32[2]{0:T(128)S(1)} %pad_add_fusion.index, bf16[4,192,896]{2,1,0:T(8,128)(2,1)} %all-to-all-done.1.own, bf16[4,896,384]{2,1,0:T(8,128)(2,1)S(1)} %shard_map.118.w), custom_call_target="tpu_custom_call" | custom-call | flops 587202560 | bytes 5439496 | tf_op jit(solution)/shard_map/pallas_call | solution.py:21
  92.2 1.9 %collective-permute-start.5 = (bf16[256,640]{1,0:T(8,128)(2,1)S(1)}, bf16[256,640]{1,0:T(8,128)(2,1)S(1)}, u32[]{:S(2)}, u32[]{:S(2)}) collective-permute-start(bf16[256,640]{1,0:T(8,128)(2,1)S(1)} %shard_map.121), channel_id=1, source_target_pairs={{0,64},{32,96},{64,0},{96,32},{1,65},{33,97},{65,1},{97,33},{2,66}... | collective-permute-start | bytes 983048 | tf_op jit(solution)/shard_map/ppermute | solution.py:45
  94.2 10.1 %collective-permute-done.5.chip = bf16[256,640]{1,0:T(8,128)(2,1)S(1)} collective-permute-done((bf16[256,640]{1,0:T(8,128)(2,1)S(1)}, bf16[256,640]{1,0:T(8,128)(2,1)S(1)}, u32[]{:S(2)}, u32[]{:S(2)}) %collective-permute-start.5) | collective-permute-done | bytes 327712 | tf_op jit(solution)/shard_map/ppermute | solution.py:45
  104.5 8.4 %all-gather = bf16[1088,384]{1,0:T(8,128)(2,1)S(1)} all-gather(bf16[272,384]{1,0:T(8,128)(2,1)S(1)} %shard_map.122), channel_id=2, replica_groups=mesh['pipe'=4,'rep'=4,'z'=8,'yh'=4] {'rep'}, dimensions={0}, use_global_device_ids=true | all-gather | bytes 1044480 | tf_op jit(solution)/shard_map/all_gather | solution.py:300
  112.9 1.2 shard_map.123
  115.1 9.4 %all-to-all-start.2 = ((bf16[32,8,1920]{2,1,0:T(8,128)(2,1)}), bf16[32,8,1920]{2,1,0:T(8,128)(2,1)S(1)}, u32[]{:S(2)}, u32[]{:S(2)}) async-start(bf16[32,8,1920]{2,1,0:T(8,128)(2,1)} %bitcast.40), calls=%async_computation.2 | async-start | bytes 1966080 | tf_op jit(solution)/shard_map/all_to_all | solution.py:305
  125.4 29.2 %all-to-all-done.2 = bf16[32,8,1920]{2,1,0:T(8,128)(2,1)S(1)} async-done(((bf16[32,8,1920]{2,1,0:T(8,128)(2,1)}), bf16[32,8,1920]{2,1,0:T(8,128)(2,1)S(1)}, u32[]{:S(2)}, u32[]{:S(2)}) %all-to-all-start.2) | async-done | bytes 983072 | tf_op jit(solution)/shard_map/all_to_all | solution.py:305
  154.6 1.2 shard_map.125
  (37 shorter events, 6.4 us)
Async XLA Ops:
  0.6 14.2 %collective-permute-start = (bf16[1,128,896]{2,1,0:T(8,128)(2,1)}, bf16[1,128,896]{2,1,0:T(8,128)(2,1)S(1)}, u32[]{:S(2)}, u32[]{:S(2)}) collective-permute-start(bf16[1,128,896]{2,1,0:T(8,128)(2,1)} %param.9), channel_id=1, source_target_pairs={{0,128},{128,256},{256,384},{384,0},{1,129},{129,257},{257,385},{3... | collective-permute-start | bytes 688136 | tf_op jit(solution)/shard_map/ppermute | solution.py:238
  4.1 1.5 copy-start
  5.6 1.2 copy-start.3
  6.8 7.0 %copy-start.7 = (s32[1,128,8]{1,2,0:T(8,128)S(1)}, s32[1,128,8]{1,2,0:T(8,128)}, u32[]{:S(2)}) copy-start(s32[1,128,8]{1,2,0:T(8,128)} %param.13) | copy-start | bytes 12292
  6.8 7.0 %copy-start.8 = (s32[1,128,8]{1,2,0:T(8,128)S(1)}, s32[1,128,8]{1,2,0:T(8,128)}, u32[]{:S(2)}) copy-start(s32[1,128,8]{1,2,0:T(8,128)} %param.12) | copy-start | bytes 12292
  6.8 7.7 %copy-start.5 = (bf16[1,128,896]{2,1,0:T(8,128)(2,1)S(1)}, bf16[1,128,896]{2,1,0:T(8,128)(2,1)}, u32[]{:S(2)}) copy-start(bf16[1,128,896]{2,1,0:T(8,128)(2,1)} %param.10) | copy-start | bytes 688132
  6.8 7.7 %copy-start.6 = (bf16[1,128,896]{2,1,0:T(8,128)(2,1)S(1)}, bf16[1,128,896]{2,1,0:T(8,128)(2,1)}, u32[]{:S(2)}) copy-start(bf16[1,128,896]{2,1,0:T(8,128)(2,1)} %param.11) | copy-start | bytes 688132
  7.5 33.6 %collective-permute-start.1 = (bf16[2,896,384]{2,1,0:T(8,128)(2,1)S(1)}, bf16[2,896,384]{2,1,0:T(8,128)(2,1)}, u32[]{:S(2)}, u32[]{:S(2)}) collective-permute-start(bf16[2,896,384]{2,1,0:T(8,128)(2,1)S(1)} %shard_map.115), channel_id=1, source_target_pairs={{0,64},{32,96},{64,0},{96,32},{1,65},{33,97},{65,1},{97,33},{2,66}... | collective-permute-start | bytes 4128776 | tf_op jit(solution)/shard_map/ppermute | solution.py:45
  15.9 26.9 %all-to-all-start = ((bf16[8,48,896]{2,1,0:T(8,128)(2,1)}), bf16[8,48,896]{2,1,0:T(8,128)(2,1)S(1)}, u32[]{:S(2)}, u32[]{:S(2)}) async-start(bf16[8,48,896]{2,1,0:T(8,128)(2,1)} %shard_map.114), calls=%async_computation | async-start | bytes 1376256 | tf_op jit(solution)/shard_map/all_to_all | solution.py:277
  44.0 7.4 %copy-start.1 = (bf16[1,1,3584,1,256]{4,2,3,1,0:T(8,128)(2,1)S(1)}, bf16[1,1,3584,1,256]{4,2,3,1,0:T(8,128)(2,1)}, u32[]{:S(2)}) copy-start(bf16[1,1,3584,1,256]{4,2,3,1,0:T(8,128)(2,1)} %param.16) | copy-start | bytes 5505028
  44.0 7.4 %copy-start.4 = (bf16[1,1,3584,1,128]{4,2,3,1,0:T(8,128)(2,1)S(1)}, bf16[1,1,3584,1,128]{4,2,3,1,0:T(8,128)(2,1)}, u32[]{:S(2)}) copy-start(bf16[1,1,3584,1,128]{4,2,3,1,0:T(8,128)(2,1)} %param.17) | copy-start | bytes 2752516
  44.0 41.4 %all-to-all-start.1 = ((bf16[4,192,896]{2,1,0:T(8,128)(2,1)}), bf16[4,192,896]{2,1,0:T(8,128)(2,1)}, u32[]{:S(2)}, u32[]{:S(2)}) async-start(bf16[4,192,896]{2,1,0:T(8,128)(2,1)} %shard_map.116), calls=%async_computation.1 | async-start | bytes 2752512 | tf_op jit(solution)/shard_map/all_to_all | solution.py:291
  52.3 5.9 %collective-permute-start.2 = (bf16[896,384]{1,0:T(8,128)(2,1)S(1)}, bf16[896,384]{1,0:T(8,128)(2,1)S(1)}, u32[]{:S(2)}, u32[]{:S(2)}) collective-permute-start(bf16[896,384]{1,0:T(8,128)(2,1)S(1)} %get-tuple-element.39), channel_id=1, source_target_pairs={{0,32},{32,0},{64,96},{96,64},{1,33},{33,1},{65,97},{97,65},{2,34}... | collective-permute-start | bytes 2064392 | tf_op jit(solution)/shard_map/ppermute | solution.py:41
  55.7 4.2 %collective-permute-start.3 = (bf16[896,384]{1,0:T(8,128)(2,1)S(1)}, bf16[896,384]{1,0:T(8,128)(2,1)S(1)}, u32[]{:S(2)}, u32[]{:S(2)}) collective-permute-start(bf16[896,384]{1,0:T(8,128)(2,1)S(1)} %get-tuple-element.37), channel_id=1, source_target_pairs={{0,32},{32,0},{64,96},{96,64},{1,33},{33,1},{65,97},{97,65},{2,34}... | collective-permute-start | bytes 2064392 | tf_op jit(solution)/shard_map/ppermute | solution.py:41
  87.8 4.4 %collective-permute-start.4 = (bf16[256,1280]{1,0:T(8,128)(2,1)S(1)}, bf16[256,1280]{1,0:T(8,128)(2,1)S(1)}, u32[]{:S(2)}, u32[]{:S(2)}) collective-permute-start(bf16[256,1280]{1,0:T(8,128)(2,1)S(1)} %shard_map.120), channel_id=1, source_target_pairs={{0,32},{32,0},{64,96},{96,64},{1,33},{33,1},{65,97},{97,65},{2,34}... | collective-permute-start | bytes 1966088 | tf_op jit(solution)/shard_map/ppermute | solution.py:41
  92.2 12.0 %collective-permute-start.5 = (bf16[256,640]{1,0:T(8,128)(2,1)S(1)}, bf16[256,640]{1,0:T(8,128)(2,1)S(1)}, u32[]{:S(2)}, u32[]{:S(2)}) collective-permute-start(bf16[256,640]{1,0:T(8,128)(2,1)S(1)} %shard_map.121), channel_id=1, source_target_pairs={{0,64},{32,96},{64,0},{96,32},{1,65},{33,97},{65,1},{97,33},{2,66}... | collective-permute-start | bytes 983048 | tf_op jit(solution)/shard_map/ppermute | solution.py:45
  114.1 1.0 copy-start.2
  115.1 9.4 %copy-start.9 = (bf16[1,128,8]{1,2,0:T(8,128)(2,1)S(1)}, bf16[1,128,8]{1,2,0:T(8,128)(2,1)}, u32[]{:S(2)}) copy-start(bf16[1,128,8]{1,2,0:T(8,128)(2,1)} %param.14) | copy-start | bytes 6148
  115.1 9.4 %copy-start.10 = (bf16[1,128,8]{1,2,0:T(8,128)(2,1)S(1)}, bf16[1,128,8]{1,2,0:T(8,128)(2,1)}, u32[]{:S(2)}) copy-start(bf16[1,128,8]{1,2,0:T(8,128)(2,1)} %param.15) | copy-start | bytes 6148
  115.1 39.5 %all-to-all-start.2 = ((bf16[32,8,1920]{2,1,0:T(8,128)(2,1)}), bf16[32,8,1920]{2,1,0:T(8,128)(2,1)S(1)}, u32[]{:S(2)}, u32[]{:S(2)}) async-start(bf16[32,8,1920]{2,1,0:T(8,128)(2,1)} %bitcast.40), calls=%async_computation.2 | async-start | bytes 1966080 | tf_op jit(solution)/shard_map/all_to_all | solution.py:305

commit v4 on v3

--- a/solution.py
+++ b/solution.py
@@ -151,7 +151,7 @@
 def first_kernel(index, own, w, out):
     units = w.shape[2] // 3
     n = own.shape[1] // 3
-    for i in range(2):
+    for i in range(out.shape[1] // (5 * units)):
         at = 5 * units * i
         wi, wd = w[index[i], :, : 2 * units], w[index[i], :, 2 * units :]
         for s in range(NY):
@@ -163,8 +163,7 @@
 
 
 def add_kernel(kept, core, out):
-    wide = out.shape[1]
-    out[...] = (kept[:, wide:] + core[:, wide:].astype(F32)).astype(BF16)
+    out[...] = (kept[...] + core[:, out.shape[1] :].astype(F32)).astype(BF16)
 
 
 def by_source(value):
@@ -179,7 +178,7 @@
     wide = chip.shape[1]
     units = out.shape[1] // 3
     rows = kept.shape[0]
-    v = kept[:, :wide] + core[:, :wide].astype(F32) + chip[...].astype(F32)
+    v = kept[...] + core[:, :wide].astype(F32) + chip[...].astype(F32)
     ag, au, g, u, dh = [v[:, i * units : (i + 1) * units] for i in range(5)]
     hid_a = ag * jax.nn.sigmoid(ag) * au
     sq = jax.nn.sigmoid(g)
@@ -275,7 +274,10 @@
         2 * tok * slots * dl,
     )
     z_all = lax.all_to_all(z_out, "z", 0, 0, tiled=True)
-    z_all, w_chip = lax.optimization_barrier((z_all, w_chip))
+    z_all, w_chip, ra, rb, ga, gb = lax.optimization_barrier((z_all, w_chip, ra, rb, ga, gb))
+    sel_b, wt_a, wt_b = call(
+        weights_kernel, [like((tok, 2 * slots))] * 3, [ra, rb, ga, gb], 8 * tok * tok * slots
+    )
     w_here = features(rep, rep ^ 1)
     w_core = core_swap(w_here[1])
     w_diag = core_swap(w_chip[1])
@@ -289,25 +291,25 @@
 
     own = one(spread_kernel, like((NY, 3 * n, dl)), [z_all], NY * 3 * n * dl)
     own = lax.all_to_all(own, "yh", 0, 0, tiled=True)
+    own, sel_b, wt_a, wt_b = lax.optimization_barrier((own, sel_b, wt_a, wt_b))
 
     rows, wide = NY * n, 5 * units
     work = 2 * rows * dl * 2 * wide
     core = one(first_kernel, like((rows, 2 * wide)), [own, w_all], work, [rep ^ 1, rep ^ 3])
     core = core_swap(core)
-    kept = one(first_kernel, like((rows, 2 * wide), F32), [own, w_all], work, [rep, rep ^ 2])
-    chip = chip_swap(one(add_kernel, like((rows, wide)), [kept, core], rows * wide))
+    kept = one(first_kernel, like((rows, wide), F32), [own, w_all], work // 2, [rep ^ 2])
+    to_chip = one(add_kernel, like((rows, wide)), [kept, core], rows * wide)
+    chip = chip_swap(to_chip)
+    own, to_chip = lax.optimization_barrier((own, to_chip))
+    kept = one(first_kernel, like((rows, wide), F32), [own, w_all], work // 2, [rep])
     mine = one(middle_kernel, like((rows + PAD, 3 * units)), [kept, core, chip], rows * units * 40)
     hidden = lax.all_gather(mine, "rep")
     back = one(
         last_kernel, like((rows, 2 * dl + units)), [hidden, w_all], 2 * rows * dl * 12 * units
     )
-    back, ra, rb, ga, gb = lax.optimization_barrier((back, ra, rb, ga, gb))
     back = lax.all_to_all(back.reshape(sources, CAP, -1), ("z", "yh"), 0, 0, tiled=True)
     back = back.reshape(rows, -1)
 
-    sel_b, wt_a, wt_b = call(
-        weights_kernel, [like((tok, 2 * slots))] * 3, [ra, rb, ga, gb], 8 * tok * tok * slots
-    )
     y, dx, dgate = call(
         combine_kernel,
         [like((tok, dl)), like((tok, dl)), like((routes_b.shape[2], tok))],

time: 156 us -> 154 us (0.987)
  the two profiles are of different devices: /device:TPU:8 before, /device:TPU:10 now
where the time goes in v4:
time: 154 us; the launch traced here: 153 us
  waiting for transfers between devices  51.7 us (34%)
  blocking collectives  46.9 us (30%)
  starting transfers between devices  34.8 us (23%)
  Pallas kernels  14.8 us (10%)
  local copies, waits for them, and re-layouts  4.3 us (3%)
    all_to_all x1, blocking collectives, on_device(): lax.all_to_all(back.reshape(sources, CAP, -1), ('z', 'yh'), 0, 0, tiled=T...  37.7 us
    ppermute x2, waiting for transfers between devices, chip_swap(): return lax.ppermute(value, 'rep', [(i, i ^ 2) for i in range(4)])  25.2 us
    all_to_all x1, waiting for transfers between devices, on_device(): own = lax.all_to_all(own, 'yh', 0, 0, tiled=True)  24.1 us
    pallas_call x13, Pallas kernels, call(): pl.pallas_call(kernel, out_shape=outs, in_specs=specs or [VMEM] * len(arg...  13.3 us
    all_to_all x1, starting transfers between devices, on_device(): z_all = lax.all_to_all(z_out, 'z', 0, 0, tiled=True)  10.3 us
    all_gather x1, blocking collectives, on_device(): hidden = lax.all_gather(mine, 'rep')  9.12 us
    ppermute x2, starting transfers between devices, chip_swap(): return lax.ppermute(value, 'rep', [(i, i ^ 2) for i in range(4)])  7.45 us
    all_to_all x1, starting transfers between devices, on_device(): own = lax.all_to_all(own, 'yh', 0, 0, tiled=True)  7.35 us
  transfers between devices with their start and end apart: 8, of which 6 were waited for; matrix products, arithmetic and copies ran while one was open for 1% of the time, Pallas kernels for 6%

profile of v4, /device:TPU:10, one launch (start us, length us, event | category | flops | bytes accessed | tf_op | source)
XLA Modules:
  0.0 153.5 jit_solution(13607179065564240596)
XLA Ops:
  0.6 3.4 %collective-permute-start = (bf16[1,128,896]{2,1,0:T(8,128)(2,1)}, bf16[1,128,896]{2,1,0:T(8,128)(2,1)S(1)}, u32[]{:S(2)}, u32[]{:S(2)}) collective-permute-start(bf16[1,128,896]{2,1,0:T(8,128)(2,1)} %param.9), channel_id=1, source_target_pairs={{0,128},{128,256},{256,384},{384,0},{1,129},{129,257},{257,385},{3... | collective-permute-start | bytes 688136 | tf_op jit(solution)/shard_map/ppermute | solution.py:237
  4.1 1.5 copy-done
  5.6 1.2 copy-done.2
  7.5 2.4 %collective-permute-start.1 = (bf16[2,896,384]{2,1,0:T(8,128)(2,1)S(1)}, bf16[2,896,384]{2,1,0:T(8,128)(2,1)}, u32[]{:S(2)}, u32[]{:S(2)}) collective-permute-start(bf16[2,896,384]{2,1,0:T(8,128)(2,1)S(1)} %shard_map.115), channel_id=1, source_target_pairs={{0,64},{32,96},{64,0},{96,32},{1,65},{33,97},{65,1},{97,33},{2,66}... | collective-permute-start | bytes 4128776 | tf_op jit(solution)/shard_map/ppermute | solution.py:45
  10.9 1.1 shard_map.114
  12.0 10.3 %all-to-all-start = ((bf16[8,48,896]{2,1,0:T(8,128)(2,1)}), bf16[8,48,896]{2,1,0:T(8,128)(2,1)S(1)}, u32[]{:S(2)}, u32[]{:S(2)}) async-start(bf16[8,48,896]{2,1,0:T(8,128)(2,1)} %shard_map.114), calls=%async_computation | async-start | bytes 1376256 | tf_op jit(solution)/shard_map/all_to_all | solution.py:276
  22.3 18.9 %collective-permute-done.1 = bf16[2,896,384]{2,1,0:T(8,128)(2,1)} collective-permute-done((bf16[2,896,384]{2,1,0:T(8,128)(2,1)S(1)}, bf16[2,896,384]{2,1,0:T(8,128)(2,1)}, u32[]{:S(2)}, u32[]{:S(2)}) %collective-permute-start.1) | collective-permute-done | bytes 1376288 | tf_op jit(solution)/shard_map/ppermute | solution.py:45
  41.2 1.6 %all-to-all-done.z_rows = bf16[8,48,896]{2,1,0:T(8,128)(2,1)S(1)} async-done(((bf16[8,48,896]{2,1,0:T(8,128)(2,1)}), bf16[8,48,896]{2,1,0:T(8,128)(2,1)S(1)}, u32[]{:S(2)}, u32[]{:S(2)}) %all-to-all-start) | async-done | bytes 688160 | tf_op jit(solution)/shard_map/all_to_all | solution.py:276
  42.8 1.2 shard_map.116
  44.0 7.3 %all-to-all-start.1 = ((bf16[4,192,896]{2,1,0:T(8,128)(2,1)}), bf16[4,192,896]{2,1,0:T(8,128)(2,1)}, u32[]{:S(2)}, u32[]{:S(2)}) async-start(bf16[4,192,896]{2,1,0:T(8,128)(2,1)} %shard_map.116), calls=%async_computation.1 | async-start | bytes 2752512 | tf_op jit(solution)/shard_map/all_to_all | solution.py:293
  52.3 1.9 %collective-permute-start.2 = (bf16[896,384]{1,0:T(8,128)(2,1)S(1)}, bf16[896,384]{1,0:T(8,128)(2,1)S(1)}, u32[]{:S(2)}, u32[]{:S(2)}) collective-permute-start(bf16[896,384]{1,0:T(8,128)(2,1)S(1)} %get-tuple-element.47), channel_id=1, source_target_pairs={{0,32},{32,0},{64,96},{96,64},{1,33},{33,1},{65,97},{97,65},{2,34}... | collective-permute-start | bytes 2064392 | tf_op jit(solution)/shard_map/ppermute | solution.py:41
  54.2 1.4 slice_bitcast_fusion.2
  55.7 2.4 %collective-permute-start.3 = (bf16[896,384]{1,0:T(8,128)(2,1)S(1)}, bf16[896,384]{1,0:T(8,128)(2,1)S(1)}, u32[]{:S(2)}, u32[]{:S(2)}) collective-permute-start(bf16[896,384]{1,0:T(8,128)(2,1)S(1)} %get-tuple-element.45), channel_id=1, source_target_pairs={{0,32},{32,0},{64,96},{96,64},{1,33},{33,1},{65,97},{97,65},{2,34}... | collective-permute-start | bytes 2064392 | tf_op jit(solution)/shard_map/ppermute | solution.py:41
  60.1 24.1 %all-to-all-done.1.own = bf16[4,192,896]{2,1,0:T(8,128)(2,1)} async-done(((bf16[4,192,896]{2,1,0:T(8,128)(2,1)}), bf16[4,192,896]{2,1,0:T(8,128)(2,1)}, u32[]{:S(2)}, u32[]{:S(2)}) %all-to-all-start.1) | async-done | bytes 1376288 | tf_op jit(solution)/shard_map/all_to_all | solution.py:293
  84.2 2.4 %shard_map.121 = bf16[256,1280]{1,0:T(8,128)(2,1)S(1)} custom-call(s32[2]{0:T(128)S(1)} %pad_add_fusion.2.index, bf16[4,192,896]{2,1,0:T(8,128)(2,1)} %all-to-all-done.1.own, bf16[4,896,384]{2,1,0:T(8,128)(2,1)S(1)} %shard_map.119.w), custom_call_target="tpu_custom_call" | custom-call | flops 587202560 | bytes 4784136 | tf_op jit(solution)/shard_map/pallas_call | solution.py:21
  86.6 1.9 %collective-permute-start.4 = (bf16[256,1280]{1,0:T(8,128)(2,1)S(1)}, bf16[256,1280]{1,0:T(8,128)(2,1)S(1)}, u32[]{:S(2)}, u32[]{:S(2)}) collective-permute-start(bf16[256,1280]{1,0:T(8,128)(2,1)S(1)} %shard_map.121), channel_id=1, source_target_pairs={{0,32},{32,0},{64,96},{96,64},{1,33},{33,1},{65,97},{97,65},{2,34}... | collective-permute-start | bytes 1966088 | tf_op jit(solution)/shard_map/ppermute | solution.py:41
  88.5 1.9 %shard_map.120.kept = f32[256,640]{1,0:T(8,128)S(1)} custom-call(s32[1]{0:T(128)} %bitcast.8.index, bf16[4,192,896]{2,1,0:T(8,128)(2,1)} %all-to-all-done.1.own, bf16[4,896,384]{2,1,0:T(8,128)(2,1)S(1)} %shard_map.119.w), custom_call_target="tpu_custom_call" | custom-call | flops 293601280 | bytes 4784132 | tf_op jit(solution)/shard_map/pallas_call | solution.py:21
  90.6 5.1 %collective-permute-start.5 = (bf16[256,640]{1,0:T(8,128)(2,1)S(1)}, bf16[256,640]{1,0:T(8,128)(2,1)S(1)}, u32[]{:S(2)}, u32[]{:S(2)}) collective-permute-start(bf16[256,640]{1,0:T(8,128)(2,1)S(1)} %shard_map.122), channel_id=1, source_target_pairs={{0,64},{32,96},{64,0},{96,32},{1,65},{33,97},{65,1},{97,33},{2,66}... | collective-permute-start | bytes 983048 | tf_op jit(solution)/shard_map/ppermute | solution.py:45
  95.7 1.9 %shard_map.123.kept = f32[256,640]{1,0:T(8,128)S(1)} custom-call(s32[1]{0:T(128)} %bitcast.rep.index, bf16[4,192,896]{2,1,0:T(8,128)(2,1)} %all-to-all-done.1.own, bf16[4,896,384]{2,1,0:T(8,128)(2,1)S(1)} %shard_map.119.w), custom_call_target="tpu_custom_call" | custom-call | flops 293601280 | bytes 4784132 | tf_op jit(solution)/shard_map/pallas_call | solution.py:21
  97.6 6.3 %collective-permute-done.5.chip = bf16[256,640]{1,0:T(8,128)(2,1)S(1)} collective-permute-done((bf16[256,640]{1,0:T(8,128)(2,1)S(1)}, bf16[256,640]{1,0:T(8,128)(2,1)S(1)}, u32[]{:S(2)}, u32[]{:S(2)}) %collective-permute-start.5) | collective-permute-done | bytes 327712 | tf_op jit(solution)/shard_map/ppermute | solution.py:45
  104.2 9.1 %all-gather = bf16[1088,384]{1,0:T(8,128)(2,1)S(1)} all-gather(bf16[272,384]{1,0:T(8,128)(2,1)S(1)} %shard_map.124), channel_id=2, replica_groups=mesh['pipe'=4,'rep'=4,'z'=8,'yh'=4] {'rep'}, dimensions={0}, use_global_device_ids=true | all-gather | bytes 1044480 | tf_op jit(solution)/shard_map/all_gather | solution.py:306
  113.3 1.2 shard_map.125
  114.6 37.7 %all_to_all.15 = bf16[32,8,1920]{2,1,0:T(8,128)(2,1)S(1)} all-to-all(bf16[32,8,1920]{2,1,0:T(8,128)(2,1)S(1)} %bitcast.40), channel_id=1, replica_groups=mesh['pipe'=4,'rep'=4,'z'=8,'yh'=4] {'z','yh'}, dimensions={0} | all-to-all | bytes 1966080 | tf_op jit(solution)/shard_map/all_to_all | solution.py:310
  152.3 1.2 shard_map.126
  (34 shorter events, 5.2 us)
Async XLA Ops:
  0.6 10.3 %collective-permute-start = (bf16[1,128,896]{2,1,0:T(8,128)(2,1)}, bf16[1,128,896]{2,1,0:T(8,128)(2,1)S(1)}, u32[]{:S(2)}, u32[]{:S(2)}) collective-permute-start(bf16[1,128,896]{2,1,0:T(8,128)(2,1)} %param.9), channel_id=1, source_target_pairs={{0,128},{128,256},{256,384},{384,0},{1,129},{129,257},{257,385},{3... | collective-permute-start | bytes 688136 | tf_op jit(solution)/shard_map/ppermute | solution.py:237
  4.1 1.5 copy-start
  5.6 1.2 copy-start.2
  6.8 3.1 %copy-start.6 = (s32[1,128,8]{1,2,0:T(8,128)S(1)}, s32[1,128,8]{1,2,0:T(8,128)}, u32[]{:S(2)}) copy-start(s32[1,128,8]{1,2,0:T(8,128)} %param.13) | copy-start | bytes 12292
  6.8 3.1 %copy-start.7 = (s32[1,128,8]{1,2,0:T(8,128)S(1)}, s32[1,128,8]{1,2,0:T(8,128)}, u32[]{:S(2)}) copy-start(s32[1,128,8]{1,2,0:T(8,128)} %param.12) | copy-start | bytes 12292
  6.8 3.8 %copy-start.4 = (bf16[1,128,896]{2,1,0:T(8,128)(2,1)S(1)}, bf16[1,128,896]{2,1,0:T(8,128)(2,1)}, u32[]{:S(2)}) copy-start(bf16[1,128,896]{2,1,0:T(8,128)(2,1)} %param.10) | copy-start | bytes 688132
  6.8 3.8 %copy-start.5 = (bf16[1,128,896]{2,1,0:T(8,128)(2,1)S(1)}, bf16[1,128,896]{2,1,0:T(8,128)(2,1)}, u32[]{:S(2)}) copy-start(bf16[1,128,896]{2,1,0:T(8,128)(2,1)} %param.11) | copy-start | bytes 688132
  7.5 33.6 %collective-permute-start.1 = (bf16[2,896,384]{2,1,0:T(8,128)(2,1)S(1)}, bf16[2,896,384]{2,1,0:T(8,128)(2,1)}, u32[]{:S(2)}, u32[]{:S(2)}) collective-permute-start(bf16[2,896,384]{2,1,0:T(8,128)(2,1)S(1)} %shard_map.115), channel_id=1, source_target_pairs={{0,64},{32,96},{64,0},{96,32},{1,65},{33,97},{65,1},{97,33},{2,66}... | collective-permute-start | bytes 4128776 | tf_op jit(solution)/shard_map/ppermute | solution.py:45
  12.0 30.8 %all-to-all-start = ((bf16[8,48,896]{2,1,0:T(8,128)(2,1)}), bf16[8,48,896]{2,1,0:T(8,128)(2,1)S(1)}, u32[]{:S(2)}, u32[]{:S(2)}) async-start(bf16[8,48,896]{2,1,0:T(8,128)(2,1)} %shard_map.114), calls=%async_computation | async-start | bytes 1376256 | tf_op jit(solution)/shard_map/all_to_all | solution.py:276
  44.0 7.4 %copy-start.1 = (bf16[1,1,3584,1,256]{4,2,3,1,0:T(8,128)(2,1)S(1)}, bf16[1,1,3584,1,256]{4,2,3,1,0:T(8,128)(2,1)}, u32[]{:S(2)}) copy-start(bf16[1,1,3584,1,256]{4,2,3,1,0:T(8,128)(2,1)} %param.16) | copy-start | bytes 5505028
  44.0 7.4 %copy-start.3 = (bf16[1,1,3584,1,128]{4,2,3,1,0:T(8,128)(2,1)S(1)}, bf16[1,1,3584,1,128]{4,2,3,1,0:T(8,128)(2,1)}, u32[]{:S(2)}) copy-start(bf16[1,1,3584,1,128]{4,2,3,1,0:T(8,128)(2,1)} %param.17) | copy-start | bytes 2752516
  44.0 40.2 %all-to-all-start.1 = ((bf16[4,192,896]{2,1,0:T(8,128)(2,1)}), bf16[4,192,896]{2,1,0:T(8,128)(2,1)}, u32[]{:S(2)}, u32[]{:S(2)}) async-start(bf16[4,192,896]{2,1,0:T(8,128)(2,1)} %shard_map.116), calls=%async_computation.1 | async-start | bytes 2752512 | tf_op jit(solution)/shard_map/all_to_all | solution.py:293
  52.3 5.9 %copy-start.8 = (bf16[1,128,8]{1,2,0:T(8,128)(2,1)S(1)}, bf16[1,128,8]{1,2,0:T(8,128)(2,1)}, u32[]{:S(2)}) copy-start(bf16[1,128,8]{1,2,0:T(8,128)(2,1)} %param.14) | copy-start | bytes 6148
  52.3 5.9 %copy-start.9 = (bf16[1,128,8]{1,2,0:T(8,128)(2,1)S(1)}, bf16[1,128,8]{1,2,0:T(8,128)(2,1)}, u32[]{:S(2)}) copy-start(bf16[1,128,8]{1,2,0:T(8,128)(2,1)} %param.15) | copy-start | bytes 6148
  52.3 6.8 %collective-permute-start.2 = (bf16[896,384]{1,0:T(8,128)(2,1)S(1)}, bf16[896,384]{1,0:T(8,128)(2,1)S(1)}, u32[]{:S(2)}, u32[]{:S(2)}) collective-permute-start(bf16[896,384]{1,0:T(8,128)(2,1)S(1)} %get-tuple-element.47), channel_id=1, source_target_pairs={{0,32},{32,0},{64,96},{96,64},{1,33},{33,1},{65,97},{97,65},{2,34}... | collective-permute-start | bytes 2064392 | tf_op jit(solution)/shard_map/ppermute | solution.py:41
  55.7 4.2 %collective-permute-start.3 = (bf16[896,384]{1,0:T(8,128)(2,1)S(1)}, bf16[896,384]{1,0:T(8,128)(2,1)S(1)}, u32[]{:S(2)}, u32[]{:S(2)}) collective-permute-start(bf16[896,384]{1,0:T(8,128)(2,1)S(1)} %get-tuple-element.45), channel_id=1, source_target_pairs={{0,32},{32,0},{64,96},{96,64},{1,33},{33,1},{65,97},{97,65},{2,34}... | collective-permute-start | bytes 2064392 | tf_op jit(solution)/shard_map/ppermute | solution.py:41
  86.6 4.0 %collective-permute-start.4 = (bf16[256,1280]{1,0:T(8,128)(2,1)S(1)}, bf16[256,1280]{1,0:T(8,128)(2,1)S(1)}, u32[]{:S(2)}, u32[]{:S(2)}) collective-permute-start(bf16[256,1280]{1,0:T(8,128)(2,1)S(1)} %shard_map.121), channel_id=1, source_target_pairs={{0,32},{32,0},{64,96},{96,64},{1,33},{33,1},{65,97},{97,65},{2,34}... | collective-permute-start | bytes 1966088 | tf_op jit(solution)/shard_map/ppermute | solution.py:41
  90.6 13.3 %collective-permute-start.5 = (bf16[256,640]{1,0:T(8,128)(2,1)S(1)}, bf16[256,640]{1,0:T(8,128)(2,1)S(1)}, u32[]{:S(2)}, u32[]{:S(2)}) collective-permute-start(bf16[256,640]{1,0:T(8,128)(2,1)S(1)} %shard_map.122), channel_id=1, source_target_pairs={{0,64},{32,96},{64,0},{96,32},{1,65},{33,97},{65,1},{97,33},{2,66}... | collective-permute-start | bytes 983048 | tf_op jit(solution)/shard_map/ppermute | solution.py:45

commit v5 on v4

--- a/solution.py
+++ b/solution.py
@@ -163,7 +163,7 @@
 
 
 def add_kernel(kept, core, out):
-    out[...] = (kept[...] + core[:, out.shape[1] :].astype(F32)).astype(BF16)
+    out[...] = (kept[...] + core[...].astype(F32)).astype(BF16)
 
 
 def by_source(value):
@@ -295,12 +295,13 @@
 
     rows, wide = NY * n, 5 * units
     work = 2 * rows * dl * 2 * wide
-    core = one(first_kernel, like((rows, 2 * wide)), [own, w_all], work, [rep ^ 1, rep ^ 3])
-    core = core_swap(core)
+    half = like((rows, wide))
+    core = core_swap(one(first_kernel, half, [own, w_all], work // 2, [rep ^ 3]))
     kept = one(first_kernel, like((rows, wide), F32), [own, w_all], work // 2, [rep ^ 2])
-    to_chip = one(add_kernel, like((rows, wide)), [kept, core], rows * wide)
+    to_chip = one(add_kernel, half, [kept, core], rows * wide)
     chip = chip_swap(to_chip)
     own, to_chip = lax.optimization_barrier((own, to_chip))
+    core = core_swap(one(first_kernel, half, [own, w_all], work // 2, [rep ^ 1]))
     kept = one(first_kernel, like((rows, wide), F32), [own, w_all], work // 2, [rep])
     mine = one(middle_kernel, like((rows + PAD, 3 * units)), [kept, core, chip], rows * units * 40)
     hidden = lax.all_gather(mine, "rep")

time: 154 us -> 160 us (1.039)
  blocking collectives: 46.9 us -> 49.5 us
  starting transfers between devices: 34.8 us -> 37.1 us
    all_to_all x1, blocking collectives: 37.7 us -> 40.4 us  [on_device(): lax.all_to_all(back.reshape(sources, CAP, -1), ('z', 'yh'), 0, 0, tiled=T...]
    ppermute x3 -> x4, starting transfers between devices: 6.25 us -> 8.65 us  [core_swap(): return lax.ppermute(value, 'rep', [(i, i ^ 1) for i in range(4)])]
    pallas_call x13 -> x14, Pallas kernels: 13.3 us -> 14.8 us  [call(): pl.pallas_call(kernel, out_shape=outs, in_specs=specs or [VMEM] * len(arg...]
  transfers between devices with their start and end apart: 8 -> 9, of which waited for: 6 -> 5; matrix products, arithmetic and copies ran while one was open for 1% -> 1% of each run, Pallas kernels for 6% -> 5%
where the time goes in v5:
time: 160 us
  waiting for transfers between devices  51.3 us (32%)
  blocking collectives  49.5 us (31%)
  starting transfers between devices  37.1 us (23%)
  Pallas kernels  16.2 us (10%)
  local copies, waits for them, and re-layouts  4.3 us (3%)
    all_to_all x1, blocking collectives, on_device(): lax.all_to_all(back.reshape(sources, CAP, -1), ('z', 'yh'), 0, 0, tiled=T...  40.4 us
    ppermute x2, waiting for transfers between devices, chip_swap(): return lax.ppermute(value, 'rep', [(i, i ^ 2) for i in range(4)])  24.8 us
    all_to_all x1, waiting for transfers between devices, on_device(): own = lax.all_to_all(own, 'yh', 0, 0, tiled=True)  24.1 us
    pallas_call x14, Pallas kernels, call(): pl.pallas_call(kernel, out_shape=outs, in_specs=specs or [VMEM] * len(arg...  14.8 us
    all_to_all x1, starting transfers between devices, on_device(): z_all = lax.all_to_all(z_out, 'z', 0, 0, tiled=True)  10.3 us
    all_gather x1, blocking collectives, on_device(): hidden = lax.all_gather(mine, 'rep')  9.12 us
    ppermute x4, starting transfers between devices, core_swap(): return lax.ppermute(value, 'rep', [(i, i ^ 1) for i in range(4)])  8.65 us
    ppermute x2, starting transfers between devices, chip_swap(): return lax.ppermute(value, 'rep', [(i, i ^ 2) for i in range(4)])  7.43 us
  transfers between devices with their start and end apart: 9, of which 5 were waited for; matrix products, arithmetic and copies ran while one was open for 1% of the time, Pallas kernels for 5%

profile of v5, /device:TPU:10, one launch (start us, length us, event | category | flops | bytes accessed | tf_op | source)
XLA Modules:
  0.0 159.6 jit_solution(18369894552213748576)
XLA Ops:
  0.6 3.4 %collective-permute-start = (bf16[1,128,896]{2,1,0:T(8,128)(2,1)}, bf16[1,128,896]{2,1,0:T(8,128)(2,1)S(1)}, u32[]{:S(2)}, u32[]{:S(2)}) collective-permute-start(bf16[1,128,896]{2,1,0:T(8,128)(2,1)} %param.9), channel_id=1, source_target_pairs={{0,128},{128,256},{256,384},{384,0},{1,129},{129,257},{257,385},{3... | collective-permute-start | bytes 688136 | tf_op jit(solution)/shard_map/ppermute | solution.py:237
  4.1 1.5 copy-done
  5.6 1.2 copy-done.2
  7.5 2.4 %collective-permute-start.1 = (bf16[2,896,384]{2,1,0:T(8,128)(2,1)S(1)}, bf16[2,896,384]{2,1,0:T(8,128)(2,1)}, u32[]{:S(2)}, u32[]{:S(2)}) collective-permute-start(bf16[2,896,384]{2,1,0:T(8,128)(2,1)S(1)} %shard_map.115), channel_id=1, source_target_pairs={{0,64},{32,96},{64,0},{96,32},{1,65},{33,97},{65,1},{97,33},{2,66}... | collective-permute-start | bytes 4128776 | tf_op jit(solution)/shard_map/ppermute | solution.py:45
  12.0 10.3 %all-to-all-start = ((bf16[8,48,896]{2,1,0:T(8,128)(2,1)}), bf16[8,48,896]{2,1,0:T(8,128)(2,1)S(1)}, u32[]{:S(2)}, u32[]{:S(2)}) async-start(bf16[8,48,896]{2,1,0:T(8,128)(2,1)} %shard_map.114), calls=%async_computation | async-start | bytes 1376256 | tf_op jit(solution)/shard_map/all_to_all | solution.py:276
  22.3 18.9 %collective-permute-done.1 = bf16[2,896,384]{2,1,0:T(8,128)(2,1)} collective-permute-done((bf16[2,896,384]{2,1,0:T(8,128)(2,1)S(1)}, bf16[2,896,384]{2,1,0:T(8,128)(2,1)}, u32[]{:S(2)}, u32[]{:S(2)}) %collective-permute-start.1) | collective-permute-done | bytes 1376288 | tf_op jit(solution)/shard_map/ppermute | solution.py:45
  41.2 1.6 all-to-all-done.z_rows
  42.8 1.2 shard_map.116
  44.0 7.3 %all-to-all-start.1 = ((bf16[4,192,896]{2,1,0:T(8,128)(2,1)}), bf16[4,192,896]{2,1,0:T(8,128)(2,1)}, u32[]{:S(2)}, u32[]{:S(2)}) async-start(bf16[4,192,896]{2,1,0:T(8,128)(2,1)} %shard_map.116), calls=%async_computation.1 | async-start | bytes 2752512 | tf_op jit(solution)/shard_map/all_to_all | solution.py:293
  52.3 1.9 %collective-permute-start.2 = (bf16[896,384]{1,0:T(8,128)(2,1)S(1)}, bf16[896,384]{1,0:T(8,128)(2,1)S(1)}, u32[]{:S(2)}, u32[]{:S(2)}) collective-permute-start(bf16[896,384]{1,0:T(8,128)(2,1)S(1)} %get-tuple-element.47), channel_id=1, source_target_pairs={{0,32},{32,0},{64,96},{96,64},{1,33},{33,1},{65,97},{97,65},{2,34}... | collective-permute-start | bytes 2064392 | tf_op jit(solution)/shard_map/ppermute | solution.py:41
  54.2 1.4 slice_bitcast_fusion.2
  55.7 2.4 %collective-permute-start.3 = (bf16[896,384]{1,0:T(8,128)(2,1)S(1)}, bf16[896,384]{1,0:T(8,128)(2,1)S(1)}, u32[]{:S(2)}, u32[]{:S(2)}) collective-permute-start(bf16[896,384]{1,0:T(8,128)(2,1)S(1)} %get-tuple-element.45), channel_id=1, source_target_pairs={{0,32},{32,0},{64,96},{96,64},{1,33},{33,1},{65,97},{97,65},{2,34}... | collective-permute-start | bytes 2064392 | tf_op jit(solution)/shard_map/ppermute | solution.py:41
  60.1 24.1 %all-to-all-done.1.own = bf16[4,192,896]{2,1,0:T(8,128)(2,1)} async-done(((bf16[4,192,896]{2,1,0:T(8,128)(2,1)}), bf16[4,192,896]{2,1,0:T(8,128)(2,1)}, u32[]{:S(2)}, u32[]{:S(2)}) %all-to-all-start.1) | async-done | bytes 1376288 | tf_op jit(solution)/shard_map/all_to_all | solution.py:293
  84.2 1.9 %shard_map.121 = bf16[256,640]{1,0:T(8,128)(2,1)S(1)} custom-call(s32[1]{0:T(128)} %bitcast.9.index, bf16[4,192,896]{2,1,0:T(8,128)(2,1)} %all-to-all-done.1.own, bf16[4,896,384]{2,1,0:T(8,128)(2,1)S(1)} %shard_map.119.w), custom_call_target="tpu_custom_call" | custom-call | flops 293601280 | bytes 4456452 | tf_op jit(solution)/shard_map/pallas_call | solution.py:21
  86.1 1.9 %collective-permute-start.4 = (bf16[256,640]{1,0:T(8,128)(2,1)S(1)}, bf16[256,640]{1,0:T(8,128)(2,1)S(1)}, u32[]{:S(2)}, u32[]{:S(2)}) collective-permute-start(bf16[256,640]{1,0:T(8,128)(2,1)S(1)} %shard_map.121), channel_id=1, source_target_pairs={{0,32},{32,0},{64,96},{96,64},{1,33},{33,1},{65,97},{97,65},{2,34}... | collective-permute-start | bytes 983048 | tf_op jit(solution)/shard_map/ppermute | solution.py:41
  88.0 1.9 %shard_map.120.kept = f32[256,640]{1,0:T(8,128)S(1)} custom-call(s32[1]{0:T(128)} %bitcast.8.index, bf16[4,192,896]{2,1,0:T(8,128)(2,1)} %all-to-all-done.1.own, bf16[4,896,384]{2,1,0:T(8,128)(2,1)S(1)} %shard_map.119.w), custom_call_target="tpu_custom_call" | custom-call | flops 293601280 | bytes 4784132 | tf_op jit(solution)/shard_map/pallas_call | solution.py:21
  90.0 1.9 %shard_map.124 = bf16[256,640]{1,0:T(8,128)(2,1)S(1)} custom-call(s32[1]{0:T(128)} %bitcast.16.index, bf16[4,192,896]{2,1,0:T(8,128)(2,1)} %all-to-all-done.1.own, bf16[4,896,384]{2,1,0:T(8,128)(2,1)S(1)} %shard_map.119.w), custom_call_target="tpu_custom_call" | custom-call | flops 293601280 | bytes 4456452 | tf_op jit(solution)/shard_map/pallas_call | solution.py:21
  92.0 2.4 %collective-permute-start.5 = (bf16[256,640]{1,0:T(8,128)(2,1)S(1)}, bf16[256,640]{1,0:T(8,128)(2,1)S(1)}, u32[]{:S(2)}, u32[]{:S(2)}) collective-permute-start(bf16[256,640]{1,0:T(8,128)(2,1)S(1)} %shard_map.124), channel_id=1, source_target_pairs={{0,32},{32,0},{64,96},{96,64},{1,33},{33,1},{65,97},{97,65},{2,34}... | collective-permute-start | bytes 983048 | tf_op jit(solution)/shard_map/ppermute | solution.py:41
  94.4 5.1 %collective-permute-start.6 = (bf16[256,640]{1,0:T(8,128)(2,1)S(1)}, bf16[256,640]{1,0:T(8,128)(2,1)S(1)}, u32[]{:S(2)}, u32[]{:S(2)}) collective-permute-start(bf16[256,640]{1,0:T(8,128)(2,1)S(1)} %shard_map.122), channel_id=1, source_target_pairs={{0,64},{32,96},{64,0},{96,32},{1,65},{33,97},{65,1},{97,33},{2,66}... | collective-permute-start | bytes 983048 | tf_op jit(solution)/shard_map/ppermute | solution.py:45
  99.5 1.9 %shard_map.123.kept = f32[256,640]{1,0:T(8,128)S(1)} custom-call(s32[1]{0:T(128)} %bitcast.rep.index, bf16[4,192,896]{2,1,0:T(8,128)(2,1)} %all-to-all-done.1.own, bf16[4,896,384]{2,1,0:T(8,128)(2,1)S(1)} %shard_map.119.w), custom_call_target="tpu_custom_call" | custom-call | flops 293601280 | bytes 4784132 | tf_op jit(solution)/shard_map/pallas_call | solution.py:21
  101.4 5.9 %collective-permute-done.6.chip = bf16[256,640]{1,0:T(8,128)(2,1)S(1)} collective-permute-done((bf16[256,640]{1,0:T(8,128)(2,1)S(1)}, bf16[256,640]{1,0:T(8,128)(2,1)S(1)}, u32[]{:S(2)}, u32[]{:S(2)}) %collective-permute-start.6) | collective-permute-done | bytes 327712 | tf_op jit(solution)/shard_map/ppermute | solution.py:45
  107.6 9.1 %all-gather = bf16[1088,384]{1,0:T(8,128)(2,1)S(1)} all-gather(bf16[272,384]{1,0:T(8,128)(2,1)S(1)} %shard_map.125), channel_id=2, replica_groups=mesh['pipe'=4,'rep'=4,'z'=8,'yh'=4] {'rep'}, dimensions={0}, use_global_device_ids=true | all-gather | bytes 1044480 | tf_op jit(solution)/shard_map/all_gather | solution.py:307
  116.7 1.2 shard_map.126
  118.0 40.4 %all_to_all.15 = bf16[32,8,1920]{2,1,0:T(8,128)(2,1)S(1)} all-to-all(bf16[32,8,1920]{2,1,0:T(8,128)(2,1)S(1)} %bitcast.40), channel_id=1, replica_groups=mesh['pipe'=4,'rep'=4,'z'=8,'yh'=4] {'z','yh'}, dimensions={0} | all-to-all | bytes 1966080 | tf_op jit(solution)/shard_map/all_to_all | solution.py:311
  (36 shorter events, 7.3 us)
Async XLA Ops:
  0.6 10.3 %collective-permute-start = (bf16[1,128,896]{2,1,0:T(8,128)(2,1)}, bf16[1,128,896]{2,1,0:T(8,128)(2,1)S(1)}, u32[]{:S(2)}, u32[]{:S(2)}) collective-permute-start(bf16[1,128,896]{2,1,0:T(8,128)(2,1)} %param.9), channel_id=1, source_target_pairs={{0,128},{128,256},{256,384},{384,0},{1,129},{129,257},{257,385},{3... | collective-permute-start | bytes 688136 | tf_op jit(solution)/shard_map/ppermute | solution.py:237
  4.1 1.5 copy-start
  5.6 1.2 copy-start.2
  6.8 3.1 %copy-start.6 = (s32[1,128,8]{1,2,0:T(8,128)S(1)}, s32[1,128,8]{1,2,0:T(8,128)}, u32[]{:S(2)}) copy-start(s32[1,128,8]{1,2,0:T(8,128)} %param.13) | copy-start | bytes 12292
  6.8 3.1 %copy-start.7 = (s32[1,128,8]{1,2,0:T(8,128)S(1)}, s32[1,128,8]{1,2,0:T(8,128)}, u32[]{:S(2)}) copy-start(s32[1,128,8]{1,2,0:T(8,128)} %param.12) | copy-start | bytes 12292
  6.8 3.8 %copy-start.4 = (bf16[1,128,896]{2,1,0:T(8,128)(2,1)S(1)}, bf16[1,128,896]{2,1,0:T(8,128)(2,1)}, u32[]{:S(2)}) copy-start(bf16[1,128,896]{2,1,0:T(8,128)(2,1)} %param.10) | copy-start | bytes 688132
  6.8 3.8 %copy-start.5 = (bf16[1,128,896]{2,1,0:T(8,128)(2,1)S(1)}, bf16[1,128,896]{2,1,0:T(8,128)(2,1)}, u32[]{:S(2)}) copy-start(bf16[1,128,896]{2,1,0:T(8,128)(2,1)} %param.11) | copy-start | bytes 688132
  7.5 33.6 %collective-permute-start.1 = (bf16[2,896,384]{2,1,0:T(8,128)(2,1)S(1)}, bf16[2,896,384]{2,1,0:T(8,128)(2,1)}, u32[]{:S(2)}, u32[]{:S(2)}) collective-permute-start(bf16[2,896,384]{2,1,0:T(8,128)(2,1)S(1)} %shard_map.115), channel_id=1, source_target_pairs={{0,64},{32,96},{64,0},{96,32},{1,65},{33,97},{65,1},{97,33},{2,66}... | collective-permute-start | bytes 4128776 | tf_op jit(solution)/shard_map/ppermute | solution.py:45
  12.0 30.8 %all-to-all-start = ((bf16[8,48,896]{2,1,0:T(8,128)(2,1)}), bf16[8,48,896]{2,1,0:T(8,128)(2,1)S(1)}, u32[]{:S(2)}, u32[]{:S(2)}) async-start(bf16[8,48,896]{2,1,0:T(8,128)(2,1)} %shard_map.114), calls=%async_computation | async-start | bytes 1376256 | tf_op jit(solution)/shard_map/all_to_all | solution.py:276
  44.0 7.4 %copy-start.1 = (bf16[1,1,3584,1,256]{4,2,3,1,0:T(8,128)(2,1)S(1)}, bf16[1,1,3584,1,256]{4,2,3,1,0:T(8,128)(2,1)}, u32[]{:S(2)}) copy-start(bf16[1,1,3584,1,256]{4,2,3,1,0:T(8,128)(2,1)} %param.16) | copy-start | bytes 5505028
  44.0 7.4 %copy-start.3 = (bf16[1,1,3584,1,128]{4,2,3,1,0:T(8,128)(2,1)S(1)}, bf16[1,1,3584,1,128]{4,2,3,1,0:T(8,128)(2,1)}, u32[]{:S(2)}) copy-start(bf16[1,1,3584,1,128]{4,2,3,1,0:T(8,128)(2,1)} %param.17) | copy-start | bytes 2752516
  44.0 40.2 %all-to-all-start.1 = ((bf16[4,192,896]{2,1,0:T(8,128)(2,1)}), bf16[4,192,896]{2,1,0:T(8,128)(2,1)}, u32[]{:S(2)}, u32[]{:S(2)}) async-start(bf16[4,192,896]{2,1,0:T(8,128)(2,1)} %shard_map.116), calls=%async_computation.1 | async-start | bytes 2752512 | tf_op jit(solution)/shard_map/all_to_all | solution.py:293
  52.3 5.8 %copy-start.8 = (bf16[1,128,8]{1,2,0:T(8,128)(2,1)S(1)}, bf16[1,128,8]{1,2,0:T(8,128)(2,1)}, u32[]{:S(2)}) copy-start(bf16[1,128,8]{1,2,0:T(8,128)(2,1)} %param.14) | copy-start | bytes 6148
  52.3 5.8 %copy-start.9 = (bf16[1,128,8]{1,2,0:T(8,128)(2,1)S(1)}, bf16[1,128,8]{1,2,0:T(8,128)(2,1)}, u32[]{:S(2)}) copy-start(bf16[1,128,8]{1,2,0:T(8,128)(2,1)} %param.15) | copy-start | bytes 6148
  52.3 6.7 %collective-permute-start.2 = (bf16[896,384]{1,0:T(8,128)(2,1)S(1)}, bf16[896,384]{1,0:T(8,128)(2,1)S(1)}, u32[]{:S(2)}, u32[]{:S(2)}) collective-permute-start(bf16[896,384]{1,0:T(8,128)(2,1)S(1)} %get-tuple-element.47), channel_id=1, source_target_pairs={{0,32},{32,0},{64,96},{96,64},{1,33},{33,1},{65,97},{97,65},{2,34}... | collective-permute-start | bytes 2064392 | tf_op jit(solution)/shard_map/ppermute | solution.py:41
  55.7 4.2 %collective-permute-start.3 = (bf16[896,384]{1,0:T(8,128)(2,1)S(1)}, bf16[896,384]{1,0:T(8,128)(2,1)S(1)}, u32[]{:S(2)}, u32[]{:S(2)}) collective-permute-start(bf16[896,384]{1,0:T(8,128)(2,1)S(1)} %get-tuple-element.45), channel_id=1, source_target_pairs={{0,32},{32,0},{64,96},{96,64},{1,33},{33,1},{65,97},{97,65},{2,34}... | collective-permute-start | bytes 2064392 | tf_op jit(solution)/shard_map/ppermute | solution.py:41
  86.1 3.9 %collective-permute-start.4 = (bf16[256,640]{1,0:T(8,128)(2,1)S(1)}, bf16[256,640]{1,0:T(8,128)(2,1)S(1)}, u32[]{:S(2)}, u32[]{:S(2)}) collective-permute-start(bf16[256,640]{1,0:T(8,128)(2,1)S(1)} %shard_map.121), channel_id=1, source_target_pairs={{0,32},{32,0},{64,96},{96,64},{1,33},{33,1},{65,97},{97,65},{2,34}... | collective-permute-start | bytes 983048 | tf_op jit(solution)/shard_map/ppermute | solution.py:41
  92.0 9.4 %collective-permute-start.5 = (bf16[256,640]{1,0:T(8,128)(2,1)S(1)}, bf16[256,640]{1,0:T(8,128)(2,1)S(1)}, u32[]{:S(2)}, u32[]{:S(2)}) collective-permute-start(bf16[256,640]{1,0:T(8,128)(2,1)S(1)} %shard_map.124), channel_id=1, source_target_pairs={{0,32},{32,0},{64,96},{96,64},{1,33},{33,1},{65,97},{97,65},{2,34}... | collective-permute-start | bytes 983048 | tf_op jit(solution)/shard_map/ppermute | solution.py:41
  94.4 12.9 %collective-permute-start.6 = (bf16[256,640]{1,0:T(8,128)(2,1)S(1)}, bf16[256,640]{1,0:T(8,128)(2,1)S(1)}, u32[]{:S(2)}, u32[]{:S(2)}) collective-permute-start(bf16[256,640]{1,0:T(8,128)(2,1)S(1)} %shard_map.122), channel_id=1, source_target_pairs={{0,64},{32,96},{64,0},{96,32},{1,65},{33,97},{65,1},{97,33},{2,66}... | collective-permute-start | bytes 983048 | tf_op jit(solution)/shard_map/ppermute | solution.py:45
